TPU v7x, 32 devices: a whole 2x2x4 slice. The times are simulated.
32 devices in a mesh: ax: 8 (over z, x), rad: 4 (over y, core).
Axes of the slice: x: 2, y: 2, z: 4, core: 2. Of those that a mesh axis runs over, the one named last changes fastest.
Arguments:
- forcing: float32 [32, 5, 128, 512], P(None, None, 'ax', 'rad'), may hold values from -300 to 300, as said below
- vel_axial: float32 [128, 512], P('ax', 'rad'), may hold values from 0.2 to 1
- vel_radial: float32 [128, 512], P('ax', 'rad'), may hold values from -0.4 to 0.4
- coupling: float32 [5, 5, 128, 512], P(None, None, 'ax', 'rad'), may hold values from -1.5 to 1.5
- viscosity: float32 [5], replicated, may hold values from 0.03 to 0.18
Outputs:
- basis: float32 [32, 5, 128, 512], P(None, None, 'ax', 'rad')
- r_factor: float32 [32, 32], replicated
Inputs may be any that keep to these rules, and one draw needn't show every extreme that they name: `forcing`: forcing of the linearized equations.
All inputs are finite; a program needn't handle non-finite values.
Results may differ from a plain program's by a relative error of at most 0.00024.
Values sent between devices are 32-bit elements; how exact they have to be, the bound alone decides.
A program may use at most 64 MiB of HBM per device.

v0:
```python
import jax
import jax.numpy as jnp
from jax import lax
from jax.sharding import PartitionSpec as P

STEPS = 3


time_step = 0.8


def padded_2(shard, sides, width):
    for axis, dim in sides:
        size, length = (lax.axis_size(axis), shard.shape[dim])
        up = [(i, (i + 1) % size) for i in range(size - 1)]
        down = [(j, i) for i, j in up]
        last = lax.slice_in_dim(shard, length - width, length, axis=dim)
        initial = lax.slice_in_dim(shard, 0, width, axis=dim)
        before = lax.ppermute(last, axis, up)
        after = lax.ppermute(initial, axis, down)
        shard = jnp.concatenate([before, shard, after], axis=dim)
    return shard


def combined_all(shard, axis, combine):
    everything = lax.all_gather(shard, axis)
    initial = everything[0]

    def turn(k, so_far):
        return combine(so_far, everything[k])

    return lax.fori_loop(1, lax.axis_size(axis), turn, initial)


def operate(padded, vel_axial, vel_radial, coupling, viscosity):
    center = padded[..., 2:-2, 2:-2]
    axial_up = padded[..., 3:-1, 2:-2]
    axial_down = padded[..., 1:-3, 2:-2]
    axial_far_up = padded[..., 4:, 2:-2]
    axial_far_down = padded[..., :-4, 2:-2]
    radial_up = padded[..., 2:-2, 3:-1]
    radial_down = padded[..., 2:-2, 1:-3]
    radial_far_up = padded[..., 2:-2, 4:]
    radial_far_down = padded[..., 2:-2, :-4]
    first_axial = (8.0 * (axial_up - axial_down) - (axial_far_up - axial_far_down)) / 12.0
    first_radial = (8.0 * (radial_up - radial_down) - (radial_far_up - radial_far_down)) / 12.0
    second = (
        16.0 * (axial_up + axial_down + radial_up + radial_down)
        - (axial_far_up + axial_far_down + radial_far_up + radial_far_down)
        - 60.0 * center
    ) / 12.0
    result = (
        -vel_axial * first_axial - vel_radial * first_radial + viscosity[:, None, None] * second
    )
    for source in range(coupling.shape[1]):
        result = result + coupling[:, source] * center[..., source : source + 1, :, :]
    return result


def upper_inverse(upper_factor):
    order = upper_factor.shape[0]
    identity = jnp.eye(order, dtype=jnp.float32)

    def one_row(count, inverse):
        row_index = order - 1 - count
        factor_row = lax.dynamic_slice_in_dim(upper_factor, row_index, 1, 0)
        unit_row = lax.dynamic_slice_in_dim(identity, row_index, 1, 0)
        pivot = jnp.sum(factor_row * unit_row)
        new_row = (unit_row - jnp.dot(factor_row, inverse, precision=lax.Precision.HIGHEST)) / pivot
        return lax.dynamic_update_slice_in_dim(inverse, new_row, row_index, 0)

    return lax.fori_loop(0, order, one_row, jnp.zeros((order, order), jnp.float32))


def rim_operator(field_now, vel_axial, vel_radial, coupling, viscosity):
    padded = padded_2(field_now, (("ax", 2), ("rad", 3)), 2)
    return operate(padded, vel_axial, vel_radial, coupling, viscosity)


def join_factors(first_factor, other_factor):
    summed = jnp.dot(first_factor.T, first_factor, precision=lax.Precision.HIGHEST)
    summed = summed + jnp.dot(other_factor.T, other_factor, precision=lax.Precision.HIGHEST)
    return jnp.linalg.cholesky(summed).T


def per_device(forcing, vel_axial, vel_radial, coupling, viscosity):
    vectors, variables, axial_cells, radial_cells = forcing.shape
    field_now = forcing
    for step_index in range(STEPS):
        slope_one = rim_operator(field_now, vel_axial, vel_radial, coupling, viscosity)
        middle = field_now + time_step * slope_one
        slope_two = rim_operator(middle, vel_axial, vel_radial, coupling, viscosity)
        field_now = field_now + 0.5 * time_step * (slope_one + slope_two)
    flattened = field_now.reshape(vectors, variables * axial_cells * radial_cells)
    rows_all = variables * axial_cells * radial_cells * lax.axis_size("ax") * lax.axis_size("rad")
    local_gram = jnp.dot(flattened, flattened.T, precision=lax.Precision.HIGHEST) / rows_all
    radial_gram = lax.psum(local_gram, "rad")
    start_factor = jnp.linalg.cholesky(radial_gram).T
    upper_factor = combined_all(start_factor, "ax", join_factors)
    inverse = upper_inverse(upper_factor)
    basis = jnp.dot(inverse.T, flattened, precision=lax.Precision.HIGHEST).reshape(field_now.shape)
    return (basis, upper_factor)


def solution(mesh):
    return jax.shard_map(
        per_device,
        mesh=mesh,
        in_specs=(
            P(None, None, "ax", "rad"),
            P("ax", "rad"),
            P("ax", "rad"),
            P(None, None, "ax", "rad"),
            P(),
        ),
        out_specs=(P(None, None, "ax", "rad"), P()),
        check_vma=False,
    )
```

profile of v0, /device:TPU:0, one launch (start us, length us, event | category | flops | bytes accessed | tf_op | source)
XLA Modules:
  0.0 425.4 jit_solution(12202436114027626620)
XLA Ops:
  2.8 5.5 %collective-permute-start.1 = (f32[32,5,2,128]{3,0,2,1:T(8,128)}, f32[32,5,2,128]{3,0,2,1:T(8,128)}, u32[]{:S(2)}, u32[]{:S(2)}) collective-permute-start(f32[32,5,2,128]{3,0,2,1:T(8,128)} %copy.298), channel_id=1, source_target_pairs={{0,4},{4,8},{8,12},{12,16},{16,20},{20,24},{24,28},{1,5},{5,9},{9,... | collective-permute-start | bytes 491528 | tf_op jit(solution)/shard_map/ppermute | solution.py:19
  10.3 4.3 %copy.227 = f32[32,5,16,128]{0,2,3,1:T(8,128)} copy(f32[32,5,16,128]{3,2,1,0:T(8,128)S(1)} %copy-done) | data formatting | bytes 2621440 | tf_op args[0]
  20.6 3.5 pad_maximum_fusion
  24.2 3.1 copy-done.1
  28.6 3.0 collective-permute-start.3
  36.9 6.5 %copy.229 = f32[32,5,20,128]{3,0,2,1:T(8,128)} copy(f32[32,5,20,128]{0,2,3,1:T(8,128)} %copy-done.1) | data formatting | bytes 3276800 | tf_op jit(solution)/shard_map/concatenate | solution.py:21
  47.1 8.8 %multiply_add_fusion.7 = (f32[32,5,16,128]{3,0,2,1:T(8,128)S(1)}, f32[32,5,16,128]{3,0,2,1:T(8,128)}) fusion(f32[32,5,16,128]{3,2,1,0:T(8,128)S(1)} %copy-done, f32[32,16,128]{2,0,1:T(8,128)} %copy.238, f32[5,16,128]{2,1,0:T(8,128)S(1)} %get-tuple-element.336, f32[32,16,128]{2,0,1:T(8,128)} %copy.237, f32[5,16,128]{2,1,0:T(8,128)S(1)} %get-tuple-element.337, ...), kind=kLoop, calls=%fused_computation.117 | loop fusion | flops 12779520 | bytes 12396564 | tf_op jit(solution)/shard_map/add | solution.py:91
  57.2 5.2 %collective-permute-start.5 = (f32[32,5,2,128]{3,0,2,1:T(8,128)S(1)}, f32[32,5,2,128]{3,0,2,1:T(8,128)S(1)}, u32[]{:S(2)}, u32[]{:S(2)}) collective-permute-start(f32[32,5,2,128]{3,0,2,1:T(8,128)S(1)} %get-tuple-element.322), channel_id=1, source_target_pairs={{0,4},{4,8},{8,12},{12,16},{16,20},{20,24},{24,28},{1,5},{5,9},{9,... | collective-permute-start | bytes 491528 | tf_op jit(solution)/shard_map/ppermute | solution.py:19
  65.2 4.3 %collective-permute-done.5 = f32[32,5,2,128]{3,0,2,1:T(8,128)S(1)} collective-permute-done((f32[32,5,2,128]{3,0,2,1:T(8,128)S(1)}, f32[32,5,2,128]{3,0,2,1:T(8,128)S(1)}, u32[]{:S(2)}, u32[]{:S(2)}) %collective-permute-start.5) | collective-permute-done | bytes 163872 | tf_op jit(solution)/shard_map/ppermute | solution.py:19
  78.7 3.7 collective-permute-start.7
  88.9 9.4 %multiply_add_fusion.6 = f32[32,5,16,128]{3,0,2,1:T(8,128)S(1)} fusion(f32[32,5,16,128]{3,0,2,1:T(8,128)} %get-tuple-element.276, f32[32,5,16,128]{3,0,2,1:T(8,128)} %copy-done.2, f32[32,5,20,2]{3,0,2,1:T(8,128)} %copy.241, f32[32,5,2,128]{3,0,2,1:T(8,128)} %copy-done.7, f32[32,5,2,128]{3,0,2,1:T(8,128)} %copy-done.11, f32[32,5,20,2]{3,0,2,1:T(8,128)} %copy.243, ...), kind=kLoop, calls=%fused_computation.116 | loop fusion | flops 17039360 | bytes 7153684 | tf_op jit(solution)/shard_map/add | solution.py:93
  99.6 5.2 %collective-permute-start.9 = (f32[32,5,2,128]{3,0,2,1:T(8,128)S(1)}, f32[32,5,2,128]{3,0,2,1:T(8,128)S(1)}, u32[]{:S(2)}, u32[]{:S(2)}) collective-permute-start(f32[32,5,2,128]{3,0,2,1:T(8,128)S(1)} %get-tuple-element.310), channel_id=1, source_target_pairs={{0,4},{4,8},{8,12},{12,16},{16,20},{20,24},{24,28},{1,5},{5,9},{9,... | collective-permute-start | bytes 491528 | tf_op jit(solution)/shard_map/ppermute | solution.py:19
  107.7 3.7 collective-permute-done.9
  120.1 3.0 collective-permute-start.11
  127.8 5.9 %multiply_add_fusion.4 = (f32[32,5,16,128]{3,0,2,1:T(8,128)S(1)}, f32[32,5,16,128]{3,0,2,1:T(8,128)}) fusion(f32[32,5,16,128]{3,0,2,1:T(8,128)S(1)} %multiply_add_fusion.6, f32[32,16,128]{2,0,1:T(8,128)} %get-tuple-element.316, f32[5,16,128]{2,1,0:T(8,128)S(1)} %get-tuple-element.336, f32[32,16,128]{2,0,1:T(8,128)S(1)} %get-tuple-element.313, ...), kind=kLoop, calls=%fused_computation.114 | loop fusion | flops 16711680 | bytes 5842964 | tf_op jit(solution)/shard_map/add | solution.py:91
  135.0 5.0 %collective-permute-start.13 = (f32[32,5,2,128]{3,0,2,1:T(8,128)S(1)}, f32[32,5,2,128]{3,0,2,1:T(8,128)S(1)}, u32[]{:S(2)}, u32[]{:S(2)}) collective-permute-start(f32[32,5,2,128]{3,0,2,1:T(8,128)S(1)} %get-tuple-element.308), channel_id=1, source_target_pairs={{0,4},{4,8},{8,12},{12,16},{16,20},{20,24},{24,28},{1,5},{5,9},{9,... | collective-permute-start | bytes 491528 | tf_op jit(solution)/shard_map/ppermute | solution.py:19
  142.5 4.5 %collective-permute-done.13 = f32[32,5,2,128]{3,0,2,1:T(8,128)S(1)} collective-permute-done((f32[32,5,2,128]{3,0,2,1:T(8,128)S(1)}, f32[32,5,2,128]{3,0,2,1:T(8,128)S(1)}, u32[]{:S(2)}, u32[]{:S(2)}) %collective-permute-start.13) | collective-permute-done | bytes 163872 | tf_op jit(solution)/shard_map/ppermute | solution.py:19
  156.3 3.7 collective-permute-start.15
  166.4 9.3 %multiply_add_fusion.3 = f32[32,5,16,128]{3,0,2,1:T(8,128)S(1)} fusion(f32[32,5,16,128]{3,0,2,1:T(8,128)S(1)} %multiply_add_fusion.6, f32[32,5,16,128]{3,0,2,1:T(8,128)} %get-tuple-element.274, f32[32,5,16,128]{3,0,2,1:T(8,128)} %copy-done.3, f32[32,5,20,2]{3,0,2,1:T(8,128)} %copy.250, f32[32,5,2,128]{3,0,2,1:T(8,128)} %copy-done.6, ...), kind=kLoop, calls=%fused_computation.113 | loop fusion | flops 17039360 | bytes 7153684 | tf_op jit(solution)/shard_map/add | solution.py:93
  177.1 5.0 %collective-permute-start.17 = (f32[32,5,2,128]{3,0,2,1:T(8,128)S(1)}, f32[32,5,2,128]{3,0,2,1:T(8,128)S(1)}, u32[]{:S(2)}, u32[]{:S(2)}) collective-permute-start(f32[32,5,2,128]{3,0,2,1:T(8,128)S(1)} %get-tuple-element.296), channel_id=1, source_target_pairs={{0,4},{4,8},{8,12},{12,16},{16,20},{20,24},{24,28},{1,5},{5,9},{9,... | collective-permute-start | bytes 491528 | tf_op jit(solution)/shard_map/ppermute | solution.py:19
  182.2 3.1 collective-permute-done.16
  185.2 3.7 collective-permute-done.17
  196.5 3.2 collective-permute-start.19
  205.2 5.9 %multiply_add_fusion.1 = (f32[32,5,16,128]{3,0,2,1:T(8,128)S(1)}, f32[32,5,16,128]{3,0,2,1:T(8,128)}) fusion(f32[32,5,16,128]{3,0,2,1:T(8,128)S(1)} %multiply_add_fusion.3, f32[32,16,128]{2,0,1:T(8,128)} %get-tuple-element.302, f32[5,16,128]{2,1,0:T(8,128)S(1)} %get-tuple-element.336, f32[32,16,128]{2,0,1:T(8,128)S(1)} %get-tuple-element.299, ...), kind=kLoop, calls=%fused_computation.111 | loop fusion | flops 16711680 | bytes 5842964 | tf_op jit(solution)/shard_map/add | solution.py:91
  213.1 5.0 %collective-permute-start.21 = (f32[32,5,2,128]{3,0,2,1:T(8,128)S(1)}, f32[32,5,2,128]{3,0,2,1:T(8,128)S(1)}, u32[]{:S(2)}, u32[]{:S(2)}) collective-permute-start(f32[32,5,2,128]{3,0,2,1:T(8,128)S(1)} %get-tuple-element.294), channel_id=1, source_target_pairs={{0,4},{4,8},{8,12},{12,16},{16,20},{20,24},{24,28},{1,5},{5,9},{9,... | collective-permute-start | bytes 491528 | tf_op jit(solution)/shard_map/ppermute | solution.py:19
  220.9 4.5 %collective-permute-done.21 = f32[32,5,2,128]{3,0,2,1:T(8,128)S(1)} collective-permute-done((f32[32,5,2,128]{3,0,2,1:T(8,128)S(1)}, f32[32,5,2,128]{3,0,2,1:T(8,128)S(1)}, u32[]{:S(2)}, u32[]{:S(2)}) %collective-permute-start.21) | collective-permute-done | bytes 163872 | tf_op jit(solution)/shard_map/ppermute | solution.py:19
  234.6 3.7 collective-permute-start.23
  244.7 5.2 %multiply_add_fusion = f32[32,5,16,128]{3,0,2,1:T(8,128)S(1)} fusion(f32[32,5,16,128]{3,0,2,1:T(8,128)S(1)} %multiply_add_fusion.3, f32[32,5,16,128]{3,0,2,1:T(8,128)} %get-tuple-element.272, f32[32,5,16,128]{3,0,2,1:T(8,128)S(1)} %get-tuple-element.271, f32[32,5,20,2]{3,0,2,1:T(8,128)} %copy.258, f32[32,5,2,128]{3,0,2,1:T(8,128)} %copy-done.4, ...), kind=kLoop, calls=%fused_computation.110 | loop fusion | flops 17039360 | bytes 7153684 | tf_op jit(solution)/shard_map/add | solution.py:93
  251.9 10.8 %psum.7 = f32[32,32]{0,1:T(8,128)S(1)} all-reduce(f32[32,32]{0,1:T(8,128)S(1)} %fusion.18), channel_id=1, replica_groups=mesh['ax'=8,'rad'=4] {'rad'}, use_global_device_ids=true, to_apply=%region_0.0 | all-reduce | flops 1024 | bytes 8192 | tf_op jit(solution)/shard_map/psum | solution.py:97
  267.1 30.9 %all-gather = f32[256,32]{1,0:T(8,128)S(1)} all-gather(f32[32,32]{1,0:T(8,128)S(1)} %copy.263), channel_id=2, replica_groups=mesh['ax'=8,'rad'=4] {'ax'}, dimensions={0}, use_global_device_ids=true | all-gather | bytes 36864 | tf_op jit(solution)/shard_map/all_gather | solution.py:26
  298.1 33.1 %while.30 = (s32[]{:T(128)}, f32[32,32]{0,1:T(8,128)S(1)}, f32[8,32,32]{2,1,0:T(8,128)S(1)}, s32[]{:T(128)}, s32[]{:T(128)}, /*index=5*/s32[]{:T(128)}) while((s32[]{:T(128)}, f32[32,32]{0,1:T(8,128)S(1)}, f32[8,32,32]{2,1,0:T(8,128)S(1)}, s32[]{:T(128)}, s32[]{:T(128)}, /*index=5*/s32[]{:T(128)}) %tuple.141), condition=%wide.region_4.6_spmd, body=%wide.region_3.5_spmd.sunk | while | flops 795684 | bytes 78197 | solution.py:32
  331.3 90.0 %while.31 = (s32[]{:T(128)}, f32[32,32]{1,0:T(8,128)S(1)}, f32[32,32]{1,0:T(8,128)}, f32[32,32]{1,0:T(8,128)S(1)}, s32[]{:T(128)}, /*index=5*/s32[]{:T(128)}, s32[]{:T(128)}, s32[]{:T(128)}) while((s32[]{:T(128)}, f32[32,32]{1,0:T(8,128)S(1)}, f32[32,32]{1,0:T(8,128)}, f32[32,32]{1,0:T(8,128)S(1)}, s32[]{:T(128)}, /*index=5*/s32[]{:T(128)}, ...), condition=%wide.region_7.9_spmd, body=%wide.region_5.8_spmd.sunk | while | flops 12421 | bytes 18835 | solution.py:72
  (307 shorter events, 244.6 us)
Async XLA Ops:
  0.6 9.7 %copy-start = (f32[32,5,16,128]{3,2,1,0:T(8,128)S(1)}, f32[32,5,16,128]{3,2,1,0:T(8,128)}, u32[]{:S(2)}) copy-start(f32[32,5,16,128]{3,2,1,0:T(8,128)} %param.10) | copy-start | bytes 3932164
  2.8 15.3 %collective-permute-start.1 = (f32[32,5,2,128]{3,0,2,1:T(8,128)}, f32[32,5,2,128]{3,0,2,1:T(8,128)}, u32[]{:S(2)}, u32[]{:S(2)}) collective-permute-start(f32[32,5,2,128]{3,0,2,1:T(8,128)} %copy.298), channel_id=1, source_target_pairs={{0,4},{4,8},{8,12},{12,16},{16,20},{20,24},{24,28},{1,5},{5,9},{9,... | collective-permute-start | bytes 491528 | tf_op jit(solution)/shard_map/ppermute | solution.py:19
  9.0 10.4 %collective-permute-start = (f32[32,5,2,128]{3,0,2,1:T(8,128)}, f32[32,5,2,128]{3,0,2,1:T(8,128)}, u32[]{:S(2)}, u32[]{:S(2)}) collective-permute-start(f32[32,5,2,128]{3,0,2,1:T(8,128)} %copy.297), channel_id=1, source_target_pairs={{4,0},{8,4},{12,8},{16,12},{20,16},{24,20},{28,24},{5,1},{9,5},{13... | collective-permute-start | bytes 491528 | tf_op jit(solution)/shard_map/ppermute | solution.py:20
  18.1 28.9 %copy-start.16 = (f32[5]{0:T(128)}, f32[5]{0:T(128)S(1)}, u32[]{:S(2)}) copy-start(f32[5]{0:T(128)S(1)} %broadcast_multiply_fusion.1) | copy-start | bytes 64
  27.3 16.1 %collective-permute-start.2 = (f32[32,5,20,2]{0,2,3,1:T(8,128)S(1)}, f32[32,5,20,2]{0,2,3,1:T(8,128)S(1)}, u32[]{:S(2)}, u32[]{:S(2)}) collective-permute-start(f32[32,5,20,2]{0,2,3,1:T(8,128)S(1)} %get-tuple-element.277), channel_id=1, source_target_pairs={{1,0},{2,1},{3,2},{5,4},{6,5},{7,6},{9,8},{10,9},{11,10},{13,12},{... | collective-permute-start | bytes 76808 | tf_op jit(solution)/shard_map/ppermute | solution.py:20
  28.6 16.7 %collective-permute-start.3 = (f32[32,5,20,2]{0,2,3,1:T(8,128)S(1)}, f32[32,5,20,2]{0,2,3,1:T(8,128)S(1)}, u32[]{:S(2)}, u32[]{:S(2)}) collective-permute-start(f32[32,5,20,2]{0,2,3,1:T(8,128)S(1)} %get-tuple-element.278), channel_id=1, source_target_pairs={{0,1},{1,2},{2,3},{4,5},{5,6},{6,7},{8,9},{9,10},{10,11},{12,13},{... | collective-permute-start | bytes 76808 | tf_op jit(solution)/shard_map/ppermute | solution.py:19
  55.9 26.5 %copy-start.2 = (f32[32,5,16,128]{3,0,2,1:T(8,128)}, f32[32,5,16,128]{3,0,2,1:T(8,128)S(1)}, u32[]{:S(2)}) copy-start(f32[32,5,16,128]{3,0,2,1:T(8,128)S(1)} %get-tuple-element.275) | copy-start | bytes 3932164
  55.9 9.2 %collective-permute-start.4 = (f32[32,5,2,128]{3,0,2,1:T(8,128)S(1)}, f32[32,5,2,128]{3,0,2,1:T(8,128)S(1)}, u32[]{:S(2)}, u32[]{:S(2)}) collective-permute-start(f32[32,5,2,128]{3,0,2,1:T(8,128)S(1)} %get-tuple-element.323), channel_id=1, source_target_pairs={{4,0},{8,4},{12,8},{16,12},{20,16},{24,20},{28,24},{5,1},{9,5},{13... | collective-permute-start | bytes 491528 | tf_op jit(solution)/shard_map/ppermute | solution.py:20
  57.2 12.2 %collective-permute-start.5 = (f32[32,5,2,128]{3,0,2,1:T(8,128)S(1)}, f32[32,5,2,128]{3,0,2,1:T(8,128)S(1)}, u32[]{:S(2)}, u32[]{:S(2)}) collective-permute-start(f32[32,5,2,128]{3,0,2,1:T(8,128)S(1)} %get-tuple-element.322), channel_id=1, source_target_pairs={{0,4},{4,8},{8,12},{12,16},{16,20},{20,24},{24,28},{1,5},{5,9},{9,... | collective-permute-start | bytes 491528 | tf_op jit(solution)/shard_map/ppermute | solution.py:19
  65.2 4.4 %copy-start.7 = (f32[32,5,2,128]{3,0,2,1:T(8,128)}, f32[32,5,2,128]{3,0,2,1:T(8,128)S(1)}, u32[]{:S(2)}) copy-start(f32[32,5,2,128]{3,0,2,1:T(8,128)S(1)} %collective-permute-done.4) | copy-start | bytes 491524
  74.5 8.8 %collective-permute-start.6 = (f32[32,5,20,2]{0,2,3,1:T(8,128)S(1)}, f32[32,5,20,2]{0,2,3,1:T(8,128)}, u32[]{:S(2)}, u32[]{:S(2)}) collective-permute-start(f32[32,5,20,2]{0,2,3,1:T(8,128)S(1)} %copy.277), channel_id=1, source_target_pairs={{1,0},{2,1},{3,2},{5,4},{6,5},{7,6},{9,8},{10,9},{11,10},{13,12},{... | collective-permute-start | bytes 76808 | tf_op jit(solution)/shard_map/ppermute | solution.py:20
  78.7 7.4 %collective-permute-start.7 = (f32[32,5,20,2]{0,2,3,1:T(8,128)}, f32[32,5,20,2]{0,2,3,1:T(8,128)}, u32[]{:S(2)}, u32[]{:S(2)}) collective-permute-start(f32[32,5,20,2]{0,2,3,1:T(8,128)} %copy.278), channel_id=1, source_target_pairs={{0,1},{1,2},{2,3},{4,5},{5,6},{6,7},{8,9},{9,10},{10,11},{12,13},{... | collective-permute-start | bytes 76808 | tf_op jit(solution)/shard_map/ppermute | solution.py:19
  98.3 9.4 %collective-permute-start.8 = (f32[32,5,2,128]{3,0,2,1:T(8,128)S(1)}, f32[32,5,2,128]{3,0,2,1:T(8,128)S(1)}, u32[]{:S(2)}, u32[]{:S(2)}) collective-permute-start(f32[32,5,2,128]{3,0,2,1:T(8,128)S(1)} %get-tuple-element.311), channel_id=1, source_target_pairs={{4,0},{8,4},{12,8},{16,12},{20,16},{24,20},{28,24},{5,1},{9,5},{13... | collective-permute-start | bytes 491528 | tf_op jit(solution)/shard_map/ppermute | solution.py:20
  99.6 11.8 %collective-permute-start.9 = (f32[32,5,2,128]{3,0,2,1:T(8,128)S(1)}, f32[32,5,2,128]{3,0,2,1:T(8,128)S(1)}, u32[]{:S(2)}, u32[]{:S(2)}) collective-permute-start(f32[32,5,2,128]{3,0,2,1:T(8,128)S(1)} %get-tuple-element.310), channel_id=1, source_target_pairs={{0,4},{4,8},{8,12},{12,16},{16,20},{20,24},{24,28},{1,5},{5,9},{9,... | collective-permute-start | bytes 491528 | tf_op jit(solution)/shard_map/ppermute | solution.py:19
  107.7 3.8 copy-start.8
  116.6 7.5 %collective-permute-start.10 = (f32[32,5,20,2]{0,2,3,1:T(8,128)S(1)}, f32[32,5,20,2]{0,2,3,1:T(8,128)S(1)}, u32[]{:S(2)}, u32[]{:S(2)}) collective-permute-start(f32[32,5,20,2]{0,2,3,1:T(8,128)S(1)} %copy.279), channel_id=1, source_target_pairs={{1,0},{2,1},{3,2},{5,4},{6,5},{7,6},{9,8},{10,9},{11,10},{13,12},{... | collective-permute-start | bytes 76808 | tf_op jit(solution)/shard_map/ppermute | solution.py:20
  120.1 5.8 %collective-permute-start.11 = (f32[32,5,20,2]{0,2,3,1:T(8,128)S(1)}, f32[32,5,20,2]{0,2,3,1:T(8,128)S(1)}, u32[]{:S(2)}, u32[]{:S(2)}) collective-permute-start(f32[32,5,20,2]{0,2,3,1:T(8,128)S(1)} %copy.280), channel_id=1, source_target_pairs={{0,1},{1,2},{2,3},{4,5},{5,6},{6,7},{8,9},{9,10},{10,11},{12,13},{... | collective-permute-start | bytes 76808 | tf_op jit(solution)/shard_map/ppermute | solution.py:19
  133.7 26.3 %copy-start.3 = (f32[32,5,16,128]{3,0,2,1:T(8,128)}, f32[32,5,16,128]{3,0,2,1:T(8,128)S(1)}, u32[]{:S(2)}) copy-start(f32[32,5,16,128]{3,0,2,1:T(8,128)S(1)} %get-tuple-element.273) | copy-start | bytes 3932164
  133.7 8.8 %collective-permute-start.12 = (f32[32,5,2,128]{3,0,2,1:T(8,128)S(1)}, f32[32,5,2,128]{3,0,2,1:T(8,128)S(1)}, u32[]{:S(2)}, u32[]{:S(2)}) collective-permute-start(f32[32,5,2,128]{3,0,2,1:T(8,128)S(1)} %get-tuple-element.309), channel_id=1, source_target_pairs={{4,0},{8,4},{12,8},{16,12},{20,16},{24,20},{28,24},{5,1},{9,5},{13... | collective-permute-start | bytes 491528 | tf_op jit(solution)/shard_map/ppermute | solution.py:20
  135.0 12.0 %collective-permute-start.13 = (f32[32,5,2,128]{3,0,2,1:T(8,128)S(1)}, f32[32,5,2,128]{3,0,2,1:T(8,128)S(1)}, u32[]{:S(2)}, u32[]{:S(2)}) collective-permute-start(f32[32,5,2,128]{3,0,2,1:T(8,128)S(1)} %get-tuple-element.308), channel_id=1, source_target_pairs={{0,4},{4,8},{8,12},{12,16},{16,20},{20,24},{24,28},{1,5},{5,9},{9,... | collective-permute-start | bytes 491528 | tf_op jit(solution)/shard_map/ppermute | solution.py:19
  142.5 4.6 %copy-start.6 = (f32[32,5,2,128]{3,0,2,1:T(8,128)}, f32[32,5,2,128]{3,0,2,1:T(8,128)S(1)}, u32[]{:S(2)}) copy-start(f32[32,5,2,128]{3,0,2,1:T(8,128)S(1)} %collective-permute-done.12) | copy-start | bytes 491524
  152.1 8.8 %collective-permute-start.14 = (f32[32,5,20,2]{0,2,3,1:T(8,128)S(1)}, f32[32,5,20,2]{0,2,3,1:T(8,128)}, u32[]{:S(2)}, u32[]{:S(2)}) collective-permute-start(f32[32,5,20,2]{0,2,3,1:T(8,128)S(1)} %copy.281), channel_id=1, source_target_pairs={{1,0},{2,1},{3,2},{5,4},{6,5},{7,6},{9,8},{10,9},{11,10},{13,12},{... | collective-permute-start | bytes 76808 | tf_op jit(solution)/shard_map/ppermute | solution.py:20
  156.3 7.4 %collective-permute-start.15 = (f32[32,5,20,2]{0,2,3,1:T(8,128)}, f32[32,5,20,2]{0,2,3,1:T(8,128)}, u32[]{:S(2)}, u32[]{:S(2)}) collective-permute-start(f32[32,5,20,2]{0,2,3,1:T(8,128)} %copy.282), channel_id=1, source_target_pairs={{0,1},{1,2},{2,3},{4,5},{5,6},{6,7},{8,9},{9,10},{10,11},{12,13},{... | collective-permute-start | bytes 76808 | tf_op jit(solution)/shard_map/ppermute | solution.py:19
  175.8 9.4 %collective-permute-start.16 = (f32[32,5,2,128]{3,0,2,1:T(8,128)S(1)}, f32[32,5,2,128]{3,0,2,1:T(8,128)S(1)}, u32[]{:S(2)}, u32[]{:S(2)}) collective-permute-start(f32[32,5,2,128]{3,0,2,1:T(8,128)S(1)} %get-tuple-element.297), channel_id=1, source_target_pairs={{4,0},{8,4},{12,8},{16,12},{20,16},{24,20},{28,24},{5,1},{9,5},{13... | collective-permute-start | bytes 491528 | tf_op jit(solution)/shard_map/ppermute | solution.py:20
  177.1 11.8 %collective-permute-start.17 = (f32[32,5,2,128]{3,0,2,1:T(8,128)S(1)}, f32[32,5,2,128]{3,0,2,1:T(8,128)S(1)}, u32[]{:S(2)}, u32[]{:S(2)}) collective-permute-start(f32[32,5,2,128]{3,0,2,1:T(8,128)S(1)} %get-tuple-element.296), channel_id=1, source_target_pairs={{0,4},{4,8},{8,12},{12,16},{16,20},{20,24},{24,28},{1,5},{5,9},{9,... | collective-permute-start | bytes 491528 | tf_op jit(solution)/shard_map/ppermute | solution.py:19
  193.7 6.9 %collective-permute-start.18 = (f32[32,5,20,2]{0,2,3,1:T(8,128)S(1)}, f32[32,5,20,2]{0,2,3,1:T(8,128)}, u32[]{:S(2)}, u32[]{:S(2)}) collective-permute-start(f32[32,5,20,2]{0,2,3,1:T(8,128)S(1)} %copy.283), channel_id=1, source_target_pairs={{1,0},{2,1},{3,2},{5,4},{6,5},{7,6},{9,8},{10,9},{11,10},{13,12},{... | collective-permute-start | bytes 76808 | tf_op jit(solution)/shard_map/ppermute | solution.py:20
  196.5 6.9 %collective-permute-start.19 = (f32[32,5,20,2]{0,2,3,1:T(8,128)}, f32[32,5,20,2]{0,2,3,1:T(8,128)S(1)}, u32[]{:S(2)}, u32[]{:S(2)}) collective-permute-start(f32[32,5,20,2]{0,2,3,1:T(8,128)} %copy.284), channel_id=1, source_target_pairs={{0,1},{1,2},{2,3},{4,5},{5,6},{6,7},{8,9},{9,10},{10,11},{12,13},{... | collective-permute-start | bytes 76808 | tf_op jit(solution)/shard_map/ppermute | solution.py:19
  211.8 9.0 %collective-permute-start.20 = (f32[32,5,2,128]{3,0,2,1:T(8,128)}, f32[32,5,2,128]{3,0,2,1:T(8,128)S(1)}, u32[]{:S(2)}, u32[]{:S(2)}) collective-permute-start(f32[32,5,2,128]{3,0,2,1:T(8,128)} %get-tuple-element.295), channel_id=1, source_target_pairs={{4,0},{8,4},{12,8},{16,12},{20,16},{24,20},{28,24},{5,1},{9,5},{13... | collective-permute-start | bytes 491528 | tf_op jit(solution)/shard_map/ppermute | solution.py:20
  213.1 12.2 %collective-permute-start.21 = (f32[32,5,2,128]{3,0,2,1:T(8,128)S(1)}, f32[32,5,2,128]{3,0,2,1:T(8,128)S(1)}, u32[]{:S(2)}, u32[]{:S(2)}) collective-permute-start(f32[32,5,2,128]{3,0,2,1:T(8,128)S(1)} %get-tuple-element.294), channel_id=1, source_target_pairs={{0,4},{4,8},{8,12},{12,16},{16,20},{20,24},{24,28},{1,5},{5,9},{9,... | collective-permute-start | bytes 491528 | tf_op jit(solution)/shard_map/ppermute | solution.py:19
  220.8 4.6 %copy-start.4 = (f32[32,5,2,128]{3,0,2,1:T(8,128)}, f32[32,5,2,128]{3,0,2,1:T(8,128)S(1)}, u32[]{:S(2)}) copy-start(f32[32,5,2,128]{3,0,2,1:T(8,128)S(1)} %collective-permute-done.20) | copy-start | bytes 491524
  230.5 8.7 %collective-permute-start.22 = (f32[32,5,20,2]{0,2,3,1:T(8,128)S(1)}, f32[32,5,20,2]{0,2,3,1:T(8,128)}, u32[]{:S(2)}, u32[]{:S(2)}) collective-permute-start(f32[32,5,20,2]{0,2,3,1:T(8,128)S(1)} %copy.285), channel_id=1, source_target_pairs={{1,0},{2,1},{3,2},{5,4},{6,5},{7,6},{9,8},{10,9},{11,10},{13,12},{... | collective-permute-start | bytes 76808 | tf_op jit(solution)/shard_map/ppermute | solution.py:20
  234.6 7.3 %collective-permute-start.23 = (f32[32,5,20,2]{0,2,3,1:T(8,128)}, f32[32,5,20,2]{0,2,3,1:T(8,128)}, u32[]{:S(2)}, u32[]{:S(2)}) collective-permute-start(f32[32,5,20,2]{0,2,3,1:T(8,128)} %copy.286), channel_id=1, source_target_pairs={{0,1},{1,2},{2,3},{4,5},{5,6},{6,7},{8,9},{9,10},{10,11},{12,13},{... | collective-permute-start | bytes 76808 | tf_op jit(solution)/shard_map/ppermute | solution.py:19
  (16 other events, 29.4 us)
where the time goes:
time: 429 us; the launch traced here: 425 us
  other arithmetic  125 us (29%)
  local copies, waits for them, and re-layouts  104 us (24%)
  starting transfers between devices  66.8 us (16%)
  matrix products  52 us (12%)
  blocking collectives  41.7 us (10%)
  waiting for transfers between devices  34.1 us (8%)
    ppermute x12, starting transfers between devices, padded_2(): before = lax.ppermute(last, axis, up)  51.3 us
    dot_general x32, matrix products, one_row(): jnp.dot(factor_row, inverse, precision=lax.Precision.HIGHEST)  46.9 us
    unnamed x66, local copies, waits for them, and re-layouts  41.9 us
    reduce_sum x32, other arithmetic, one_row(): pivot = jnp.sum(factor_row * unit_row)  41.6 us
    all_gather x1, blocking collectives, combined_all(): everything = lax.all_gather(shard, axis)  30.9 us
    another operation x21, other arithmetic, join_factors(): return jnp.linalg.cholesky(summed).T  25.2 us
    add x3, other arithmetic, per_device(): field_now = field_now + 0.5 * time_step * (slope_one + slope_two)  24 us
    ppermute x12, waiting for transfers between devices, padded_2(): before = lax.ppermute(last, axis, up)  20.7 us
  transfers between devices with their start and end apart: 24, of which 10 were waited for; matrix products, arithmetic and copies ran while one was open for 12% of the time, Pallas kernels for 0%

commit v1 on v0

v1 whole, which is shorter than its diff:
```python
import functools

import jax
import jax.numpy as jnp
from jax import lax
from jax.experimental import pallas as pl
from jax.experimental.pallas import tpu as pltpu
from jax.sharding import PartitionSpec as P

STEPS = 3
time_step = 0.8

LANES = 128
SUB = 8
MESH = pl.DeviceIdType.MESH


def kernel(
    sizes, f_ref, va_ref, vr_ref, cp_ref, nu_ref, out_ref, r_ref,
    field, coef, packed, from_left, from_right, split, mine, rad_slots, ax_slots,
    send_sem, recv_sem, rad_send, rad_recv, ax_send, ax_recv,
):
    vectors, variables, rows, n_ax, n_rad = sizes
    groups = vectors // SUB
    cells = variables * rows
    ax = lax.axis_index("ax")
    rad = lax.axis_index("rad")
    ax_before = lax.rem(ax + n_ax - 1, n_ax)
    ax_after = lax.rem(ax + 1, n_ax)
    rad_before = lax.rem(rad + n_rad - 1, n_rad)
    rad_after = lax.rem(rad + 1, n_rad)
    sends = (ax > 0, ax < n_ax - 1, rad > 0, rad < n_rad - 1)
    takes = (ax < n_ax - 1, ax > 0, rad < n_rad - 1, rad > 0)
    lane = lax.broadcasted_iota(jnp.int32, (SUB, LANES), 1)
    sub = lax.broadcasted_iota(jnp.int32, (SUB, LANES), 0)
    slot = lane // 8
    tile = (SUB, LANES)

    def link(buf, g, d):
        if d == 0:
            src, dst = field.at[buf, g, :, 2:4], field.at[buf, g, :, rows + 2 : rows + 4]
            device = (ax_before, rad)
        elif d == 1:
            src, dst = field.at[buf, g, :, rows : rows + 2], field.at[buf, g, :, 0:2]
            device = (ax_after, rad)
        elif d == 2:
            src, dst = packed.at[buf, g], from_right.at[buf, g]
            device = (ax, rad_before)
        else:
            src, dst = packed.at[buf, g], from_left.at[buf, g]
            device = (ax, rad_after)
        return pltpu.make_async_remote_copy(
            src_ref=src, dst_ref=dst,
            send_sem=send_sem.at[buf, g, d], recv_sem=recv_sem.at[buf, g, d],
            device_id=device, device_id_type=MESH,
        )

    def start(buf, g, d):
        @pl.when(sends[d])
        def _():
            link(buf, g, d).start()

    def wait_send(buf, g, d):
        @pl.when(sends[d])
        def _():
            link(buf, g, d).wait_send()

    def wait_recv(buf, g, d):
        @pl.when(takes[d])
        def _():
            link(buf, g, d).wait_recv()

    zero_rows = jnp.zeros((variables, 2, SUB, LANES), jnp.float32)
    zero_side = jnp.zeros((variables, SUB, LANES), jnp.float32)
    for buf in range(2):
        for g in range(groups):
            field[buf, g, :, 0:2] = zero_rows
            field[buf, g, :, rows + 2 : rows + 4] = zero_rows
            from_left[buf, g] = zero_side
            from_right[buf, g] = zero_side

    barrier = pltpu.get_barrier_semaphore()
    for step in range(1, n_ax):
        pl.semaphore_signal(
            barrier, inc=1, device_id=(lax.rem(ax + step, n_ax), rad), device_id_type=MESH
        )
    for step in range(1, n_rad):
        pl.semaphore_signal(
            barrier, inc=1, device_id=(ax, lax.rem(rad + step, n_rad)), device_id_type=MESH
        )

    def bring(g, carry):
        for v in range(variables):
            pack = jnp.zeros(tile, jnp.float32)
            for a in range(rows):
                value = f_ref[pl.ds(g * (SUB * cells) + v * rows + a, SUB, stride=cells), :]
                field[0, g, v, a + 2] = value
                pack = jnp.where(slot == a, pltpu.roll(value, 2 + 8 * a, 1), pack)
            packed[0, g, v] = pack
        return carry

    lax.fori_loop(0, groups, bring, 0)
    pl.semaphore_wait(barrier, n_ax + n_rad - 2)

    def send_first(g, carry):
        for d in range(4):
            start(0, g, d)
        return carry

    lax.fori_loop(0, groups, send_first, 0)

    def prepare(a, carry):
        vel_a = jnp.broadcast_to(va_ref[pl.ds(a, 1), :], tile) * (time_step / 12.0)
        vel_r = jnp.broadcast_to(vr_ref[pl.ds(a, 1), :], tile) * (time_step / 12.0)
        for v in range(variables):
            nu = jnp.full(tile, nu_ref[v], jnp.float32) * (time_step / 12.0)
            terms = []
            for vel in (vel_a, vel_r):
                terms += [16.0 * nu - 8.0 * vel, 16.0 * nu + 8.0 * vel, vel - nu, -vel - nu]
            for w in range(variables):
                term = time_step * jnp.broadcast_to(cp_ref[v, w, pl.ds(a, 1), :], tile)
                if w == v:
                    term = term + (1.0 - 60.0 * nu)
                terms.append(term)
            for t, term in enumerate(terms):
                coef[v, a, t] = term
        return carry

    lax.fori_loop(0, rows, prepare, 0)

    def advance(src, g, start_axial):
        dst = 1 - src
        sides = [
            jnp.where(lane % 8 < 2, from_left[src, g, v], from_right[src, g, v])
            for v in range(variables)
        ]
        packs = [jnp.zeros(tile, jnp.float32) for _ in range(variables)]
        order = [0, 1, rows - 2, rows - 1] + list(range(2, rows - 2))
        for count, a in enumerate(order):
            centre = [field[src, g, v, a + 2] for v in range(variables)]
            for v in range(variables):
                x = centre[v]
                side = pltpu.roll(sides[v], (2 * LANES - 2 - 8 * a) % LANES, 1)
                near = [
                    field[src, g, v, a + 3],
                    field[src, g, v, a + 1],
                    field[src, g, v, a + 4],
                    field[src, g, v, a],
                    pltpu.roll(jnp.where(lane == 0, side, x), LANES - 1, 1),
                    pltpu.roll(jnp.where(lane == LANES - 1, side, x), 1, 1),
                    pltpu.roll(jnp.where(lane < 2, side, x), LANES - 2, 1),
                    pltpu.roll(jnp.where(lane >= LANES - 2, side, x), 2, 1),
                ]
                parts = [coef[v, a, t] * q for t, q in enumerate(near + centre)]
                while len(parts) > 1:
                    parts = [
                        parts[i] + parts[i + 1] if i + 1 < len(parts) else parts[i]
                        for i in range(0, len(parts), 2)
                    ]
                new = parts[0]
                if src == 1:
                    new = 0.5 * (field[dst, g, v, a + 2] + new)
                field[dst, g, v, a + 2] = new
                packs[v] = jnp.where(slot == a, pltpu.roll(new, 2 + 8 * a, 1), packs[v])
            if count == 3:
                start_axial()
        for v in range(variables):
            packed[dst, g, v] = packs[v]

    def both_halves(step, carry):
        def half(src):
            more = jnp.logical_or(step < STEPS - 1, src == 0)

            def one_group(g, inner):
                for d in range(4):
                    wait_recv(src, g, d)
                for d in range(4):
                    wait_send(src, g, d)

                def send(directions):
                    @pl.when(more)
                    def _():
                        for d in directions:
                            start(1 - src, g, d)

                advance(src, g, lambda: send((0, 1)))
                send((2, 3))
                return inner

            lax.fori_loop(0, groups, one_group, 0)

        half(0)
        half(1)
        return carry

    lax.fori_loop(0, STEPS, both_halves, 0)

    def products(v, total):
        for p in range(rows // 2):
            for e in range(2):
                x = jnp.concatenate(
                    [field[0, g, v, 2 * p + e + 2] for g in range(groups)], axis=0
                )
                high = x.astype(jnp.bfloat16)
                low = (x - high.astype(jnp.float32)).astype(jnp.bfloat16)
                split[v, p, :, e * LANES : (e + 1) * LANES] = jnp.concatenate(
                    [high, low, high, low], axis=0
                )
            both = split[v, p]
            total = total + lax.dot_general(
                both[: 2 * vectors], both, (((1,), (1,)), ((), ())),
                preferred_element_type=jnp.float32,
            )
        return total

    total = lax.fori_loop(
        0, variables, products, jnp.zeros((2 * vectors, LANES), jnp.float32)
    )
    half_sum = total[:vectors] + total[vectors:]
    gram = half_sum + pltpu.roll(half_sum, vectors, 1)
    gram = gram * (1.0 / (cells * LANES * n_ax * n_rad))
    quarter = lane // vectors
    folded = gram[:SUB]
    for i in range(1, vectors // SUB):
        folded = jnp.where(quarter == i, gram[SUB * i : SUB * (i + 1)], folded)

    def sum_over(value, n, me, place, slots, sends_on, takes_on, held):
        held[...] = value
        copies = []
        for step in range(1, n):
            copy = pltpu.make_async_remote_copy(
                src_ref=held, dst_ref=slots.at[me],
                send_sem=sends_on.at[step], recv_sem=takes_on.at[step],
                device_id=place(lax.rem(me + step, n)), device_id_type=MESH,
            )
            copy.start()
            copies.append(copy)
        slots[me] = value
        for copy in copies:
            copy.wait_send()
            copy.wait_recv()
        result = slots[0]
        for i in range(1, n):
            result = result + slots[i]
        return result

    folded = sum_over(
        folded, n_rad, rad, lambda i: (ax, i), rad_slots, rad_send, rad_recv, mine.at[0]
    )
    folded = sum_over(
        folded, n_ax, ax, lambda i: (i, rad), ax_slots, ax_send, ax_recv, mine.at[1]
    )

    blocks = []
    for b in range(vectors // SUB):
        part = folded if b == 0 else pltpu.roll(folded, LANES - vectors * b, 1)
        unit = jnp.where(lane - vectors == sub + SUB * b, 1.0, 0.0)
        blocks.append(jnp.where(lane < vectors, part, unit))
    for j in range(vectors):
        jb, js = j // SUB, j % SUB
        row = jnp.broadcast_to(blocks[jb][js : js + 1, :], tile)
        columns = {
            b: jnp.broadcast_to(blocks[b][:, j : j + 1], tile) for b in range(jb, len(blocks))
        }
        pivot = jnp.broadcast_to(columns[jb][js : js + 1, :], tile)
        scaled = row * (1.0 / pivot)
        for b in range(jb, len(blocks)):
            change = columns[b] * scaled
            if b == jb:
                change = jnp.where(sub > js, change, 0.0)
            blocks[b] = blocks[b] - change
    lefts, rights = [], []
    for b, block in enumerate(blocks):
        diagonal = jnp.sum(
            jnp.where(lane == sub + SUB * b, block, 0.0), axis=1, keepdims=True
        )
        block = block * (1.0 / jnp.sqrt(jnp.broadcast_to(diagonal, tile)))
        lefts.append(jnp.where(lane >= sub + SUB * b, block, 0.0))
        inverse = jnp.where(quarter == 1, block, 0.0)
        inverse = inverse + pltpu.roll(inverse, vectors, 1)
        inverse = inverse + pltpu.roll(inverse, 2 * vectors, 1)
        rights.append(inverse)
    r_ref[...] = jnp.concatenate(lefts, axis=0)[:, :vectors]
    inverse = jnp.concatenate(rights, axis=0)
    high = inverse.astype(jnp.bfloat16).astype(jnp.float32)
    wide = lax.broadcasted_iota(jnp.int32, (vectors, LANES), 1)
    factors = jnp.where(wide < 2 * vectors, high, inverse - high).astype(jnp.bfloat16)

    def outputs(v, carry):
        for p in range(rows // 2):
            found = jnp.dot(factors, split[v, p], preferred_element_type=jnp.float32)
            for e in range(2):
                out_ref[pl.ds(v * rows + 2 * p + e, vectors, stride=cells), :] = found[
                    :, e * LANES : (e + 1) * LANES
                ]
        return carry

    lax.fori_loop(0, variables, outputs, 0)


def per_device(forcing, vel_axial, vel_radial, coupling, viscosity):
    vectors, variables, rows, columns = forcing.shape
    n_ax, n_rad = lax.axis_size("ax"), lax.axis_size("rad")
    groups = vectors // SUB
    cells = variables * rows
    assert columns == LANES and rows * 8 == LANES and vectors * 4 == LANES
    f32 = jnp.float32
    vmem = pl.BlockSpec(memory_space=pltpu.VMEM)
    side = pltpu.VMEM((2, groups, variables, SUB, LANES), f32)
    dma = pltpu.SemaphoreType.DMA
    basis, upper = pl.pallas_call(
        functools.partial(kernel, (vectors, variables, rows, n_ax, n_rad)),
        out_shape=(
            jax.ShapeDtypeStruct((vectors * cells, LANES), f32),
            jax.ShapeDtypeStruct((vectors, vectors), f32),
        ),
        in_specs=[vmem, vmem, vmem, vmem, pl.BlockSpec(memory_space=pltpu.SMEM)],
        out_specs=(vmem, vmem),
        scratch_shapes=[
            pltpu.VMEM((2, groups, variables, rows + 4, SUB, LANES), f32),
            pltpu.VMEM((variables, rows, 8 + variables, SUB, LANES), f32),
            side, side, side,
            pltpu.VMEM((variables, rows // 2, LANES, 2 * LANES), jnp.bfloat16),
            pltpu.VMEM((2, SUB, LANES), f32),
            pltpu.VMEM((n_rad, SUB, LANES), f32),
            pltpu.VMEM((n_ax, SUB, LANES), f32),
            dma((2, groups, 4)), dma((2, groups, 4)),
            dma((n_rad,)), dma((n_rad,)), dma((n_ax,)), dma((n_ax,)),
        ],
        compiler_params=pltpu.CompilerParams(
            collective_id=0, has_side_effects=True, vmem_limit_bytes=48 * 2**20
        ),
    )(forcing.reshape(vectors * cells, LANES), vel_axial, vel_radial, coupling, viscosity)
    return basis.reshape(forcing.shape), upper


def solution(mesh):
    return jax.shard_map(
        per_device,
        mesh=mesh,
        in_specs=(
            P(None, None, "ax", "rad"),
            P("ax", "rad"),
            P("ax", "rad"),
            P(None, None, "ax", "rad"),
            P(),
        ),
        out_specs=(P(None, None, "ax", "rad"), P()),
        check_vma=False,
    )
```

time: 429 us -> 110 us (0.26)
  other arithmetic: 125 us -> 0 us
  Pallas kernels: 0 us -> 103 us
  local copies, waits for them, and re-layouts: 104 us -> 5.95 us
  starting transfers between devices: 66.8 us -> 0 us
  matrix products: 52 us -> 0 us
  blocking collectives: 41.7 us -> 0 us
  waiting for transfers between devices: 34.1 us -> 0 us
    pallas_call x0 -> x1, Pallas kernels: none -> 103 us  [per_device(): pl.pallas_call(functools.partial(kernel, (vectors, variables, rows, n_ax,...]
    ppermute x24 -> x0, starting transfers between devices: 66.8 us -> none  [the longest x12 51.3 us: padded_2(): before = lax.ppermute(last, axis, up)]
    dot_general x48 -> x0, matrix products: 52 us -> none  [the longest x32 46.9 us: one_row(): jnp.dot(factor_row, inverse, precision=lax.Precision.HIGHEST)]
    add x6 -> x0, other arithmetic: 44.5 us -> none  [the longest x3 24 us: per_device(): field_now = field_now + 0.5 * time_step * (slope_one + slope_two)]
    reduce_sum x32 -> x0, other arithmetic: 41.6 us -> none  [one_row(): pivot = jnp.sum(factor_row * unit_row)]
    unnamed x66 -> x12, local copies, waits for them, and re-layouts: 41.9 us -> 5.95 us
    ppermute x24 -> x0, waiting for transfers between devices: 34.1 us -> none  [the longest x12 20.7 us: padded_2(): before = lax.ppermute(last, axis, up)]
    all_gather x1 -> x0, blocking collectives: 30.9 us -> none  [combined_all(): everything = lax.all_gather(shard, axis)]
  transfers between devices with their start and end apart: 24 -> 0, of which waited for: 10 -> 0; matrix products, arithmetic and copies ran while one was open for 12% -> 0% of each run, Pallas kernels for 0% -> 0%
where the time goes in v1:
time: 110 us
  Pallas kernels  103 us (94%)
  local copies, waits for them, and re-layouts  5.95 us (5%)
    pallas_call x1, Pallas kernels, per_device(): pl.pallas_call(functools.partial(kernel, (vectors, variables, rows, n_ax,...  103 us
    unnamed x12, local copies, waits for them, and re-layouts  5.95 us

profile of v1, /device:TPU:0, one launch (start us, length us, event | category | flops | bytes accessed | tf_op | source)
XLA Modules:
  0.0 109.6 jit_solution(8772172718197278078)
XLA Ops:
  0.6 0.0 copy-start
  0.6 1.3 %copy-done = f32[32,5,16,128]{3,2,1,0:T(8,128)S(1)} copy-done((f32[32,5,16,128]{3,2,1,0:T(8,128)S(1)}, f32[32,5,16,128]{3,2,1,0:T(8,128)}, u32[]{:S(2)}) %copy-start) | copy-done | bytes 1310744
  1.9 0.0 copy-start.1
  2.0 0.9 copy-done.1
  2.9 0.0 copy-start.2
  2.9 0.7 copy-done.2
  3.6 0.0 copy-start.3
  3.6 0.7 copy-done.3
  4.3 0.0 copy-start.4
  4.3 0.7 copy-done.4
  4.9 103.0 %shard_map.68 = (f32[2560,128]{1,0:T(8,128)S(1)}, f32[32,32]{1,0:T(8,128)S(1)}) custom-call(f32[2560,128]{1,0:T(8,128)S(1)} %bitcast.2, f32[16,128]{1,0:T(8,128)S(1)} %copy-done.2, f32[16,128]{1,0:T(8,128)S(1)} %copy-done.3, f32[5,5,16,128]{3,2,1,0:T(8,128)S(1)} %copy-done.1, f32[5]{0:T(128)S(1)} %copy-done.4), custom_call_target="tpu_custom_call" | custom-call | tf_op jit(solution)/shard_map/pallas_call | solution.py:311
  107.9 1.1 copy.9
  109.0 0.6 copy.10
Async XLA Ops:
  0.6 1.3 %copy-start = (f32[32,5,16,128]{3,2,1,0:T(8,128)S(1)}, f32[32,5,16,128]{3,2,1,0:T(8,128)}, u32[]{:S(2)}) copy-start(f32[32,5,16,128]{3,2,1,0:T(8,128)} %param.5) | copy-start | bytes 3932164
  1.9 0.9 copy-start.1
  2.9 0.7 copy-start.2
  3.6 0.7 copy-start.3
  4.3 0.7 copy-start.4

commit v2 on v1

--- a/solution.py
+++ b/solution.py
@@ -17,12 +17,14 @@
 
 def kernel(
     sizes, f_ref, va_ref, vr_ref, cp_ref, nu_ref, out_ref, r_ref,
-    field, coef, packed, from_left, from_right, split, mine, rad_slots, ax_slots,
+    forcing_in, va_in, vr_in, cp_in, nu_in, in_sem,
+    field_0, field_1, coef, packed, from_left, from_right, split, mine, rad_slots, ax_slots,
     send_sem, recv_sem, rad_send, rad_recv, ax_send, ax_recv,
 ):
     vectors, variables, rows, n_ax, n_rad = sizes
     groups = vectors // SUB
     cells = variables * rows
+    fields = (field_0, field_1)
     ax = lax.axis_index("ax")
     rad = lax.axis_index("rad")
     ax_before = lax.rem(ax + n_ax - 1, n_ax)
@@ -38,10 +40,10 @@
 
     def link(buf, g, d):
         if d == 0:
-            src, dst = field.at[buf, g, :, 2:4], field.at[buf, g, :, rows + 2 : rows + 4]
+            src, dst = fields[buf].at[g, :, 2:4], fields[buf].at[g, :, rows + 2 : rows + 4]
             device = (ax_before, rad)
         elif d == 1:
-            src, dst = field.at[buf, g, :, rows : rows + 2], field.at[buf, g, :, 0:2]
+            src, dst = fields[buf].at[g, :, rows : rows + 2], fields[buf].at[g, :, 0:2]
             device = (ax_after, rad)
         elif d == 2:
             src, dst = packed.at[buf, g], from_right.at[buf, g]
@@ -70,12 +72,28 @@
         def _():
             link(buf, g, d).wait_recv()
 
+    part = SUB * cells
+    pieces = [
+        pltpu.make_async_copy(
+            f_ref.at[pl.ds(g * part, part)], forcing_in.at[pl.ds(g * part, part)], in_sem.at[g]
+        )
+        for g in range(groups)
+    ]
+    others = [
+        pltpu.make_async_copy(source, target, in_sem.at[groups + i])
+        for i, (source, target) in enumerate(
+            ((va_ref, va_in), (vr_ref, vr_in), (cp_ref, cp_in), (nu_ref, nu_in))
+        )
+    ]
+    for copy in pieces + others:
+        copy.start()
+
     zero_rows = jnp.zeros((variables, 2, SUB, LANES), jnp.float32)
     zero_side = jnp.zeros((variables, SUB, LANES), jnp.float32)
     for buf in range(2):
         for g in range(groups):
-            field[buf, g, :, 0:2] = zero_rows
-            field[buf, g, :, rows + 2 : rows + 4] = zero_rows
+            fields[buf][g, :, 0:2] = zero_rows
+            fields[buf][g, :, rows + 2 : rows + 4] = zero_rows
             from_left[buf, g] = zero_side
             from_right[buf, g] = zero_side
 
@@ -89,36 +107,32 @@
             barrier, inc=1, device_id=(ax, lax.rem(rad + step, n_rad)), device_id_type=MESH
         )
 
-    def bring(g, carry):
+    for g in range(groups):
+        pieces[g].wait()
         for v in range(variables):
             pack = jnp.zeros(tile, jnp.float32)
             for a in range(rows):
-                value = f_ref[pl.ds(g * (SUB * cells) + v * rows + a, SUB, stride=cells), :]
-                field[0, g, v, a + 2] = value
+                value = forcing_in[pl.ds(g * part + v * rows + a, SUB, stride=cells), :]
+                field_0[g, v, a + 2] = value
                 pack = jnp.where(slot == a, pltpu.roll(value, 2 + 8 * a, 1), pack)
             packed[0, g, v] = pack
-        return carry
-
-    lax.fori_loop(0, groups, bring, 0)
-    pl.semaphore_wait(barrier, n_ax + n_rad - 2)
-
-    def send_first(g, carry):
+        if g == 0:
+            pl.semaphore_wait(barrier, n_ax + n_rad - 2)
         for d in range(4):
             start(0, g, d)
-        return carry
-
-    lax.fori_loop(0, groups, send_first, 0)
+    for copy in others:
+        copy.wait()
 
     def prepare(a, carry):
-        vel_a = jnp.broadcast_to(va_ref[pl.ds(a, 1), :], tile) * (time_step / 12.0)
-        vel_r = jnp.broadcast_to(vr_ref[pl.ds(a, 1), :], tile) * (time_step / 12.0)
+        vel_a = jnp.broadcast_to(va_in[pl.ds(a, 1), :], tile) * (time_step / 12.0)
+        vel_r = jnp.broadcast_to(vr_in[pl.ds(a, 1), :], tile) * (time_step / 12.0)
         for v in range(variables):
-            nu = jnp.full(tile, nu_ref[v], jnp.float32) * (time_step / 12.0)
+            nu = jnp.full(tile, nu_in[v], jnp.float32) * (time_step / 12.0)
             terms = []
             for vel in (vel_a, vel_r):
                 terms += [16.0 * nu - 8.0 * vel, 16.0 * nu + 8.0 * vel, vel - nu, -vel - nu]
             for w in range(variables):
-                term = time_step * jnp.broadcast_to(cp_ref[v, w, pl.ds(a, 1), :], tile)
+                term = time_step * jnp.broadcast_to(cp_in[v, w, pl.ds(a, 1), :], tile)
                 if w == v:
                     term = term + (1.0 - 60.0 * nu)
                 terms.append(term)
@@ -130,6 +144,14 @@
 
     def advance(src, g, start_axial):
         dst = 1 - src
+        now, later = fields[src], fields[dst]
+        held = []
+
+        def store(keep):
+            while len(held) > keep:
+                v, a, value = held.pop(0)
+                later[g, v, a + 2] = value
+
         sides = [
             jnp.where(lane % 8 < 2, from_left[src, g, v], from_right[src, g, v])
             for v in range(variables)
@@ -137,15 +159,15 @@
         packs = [jnp.zeros(tile, jnp.float32) for _ in range(variables)]
         order = [0, 1, rows - 2, rows - 1] + list(range(2, rows - 2))
         for count, a in enumerate(order):
-            centre = [field[src, g, v, a + 2] for v in range(variables)]
+            centre = [now[g, v, a + 2] for v in range(variables)]
             for v in range(variables):
                 x = centre[v]
                 side = pltpu.roll(sides[v], (2 * LANES - 2 - 8 * a) % LANES, 1)
                 near = [
-                    field[src, g, v, a + 3],
-                    field[src, g, v, a + 1],
-                    field[src, g, v, a + 4],
-                    field[src, g, v, a],
+                    now[g, v, a + 3],
+                    now[g, v, a + 1],
+                    now[g, v, a + 4],
+                    now[g, v, a],
                     pltpu.roll(jnp.where(lane == 0, side, x), LANES - 1, 1),
                     pltpu.roll(jnp.where(lane == LANES - 1, side, x), 1, 1),
                     pltpu.roll(jnp.where(lane < 2, side, x), LANES - 2, 1),
@@ -159,11 +181,14 @@
                     ]
                 new = parts[0]
                 if src == 1:
-                    new = 0.5 * (field[dst, g, v, a + 2] + new)
-                field[dst, g, v, a + 2] = new
+                    new = 0.5 * (later[g, v, a + 2] + new)
+                held.append((v, a, new))
                 packs[v] = jnp.where(slot == a, pltpu.roll(new, 2 + 8 * a, 1), packs[v])
             if count == 3:
+                store(0)
                 start_axial()
+            store(2 * variables)
+        store(0)
         for v in range(variables):
             packed[dst, g, v] = packs[v]
 
@@ -199,7 +224,7 @@
         for p in range(rows // 2):
             for e in range(2):
                 x = jnp.concatenate(
-                    [field[0, g, v, 2 * p + e + 2] for g in range(groups)], axis=0
+                    [field_0[g, v, 2 * p + e + 2] for g in range(groups)], axis=0
                 )
                 high = x.astype(jnp.bfloat16)
                 low = (x - high.astype(jnp.float32)).astype(jnp.bfloat16)
@@ -307,6 +332,7 @@
     f32 = jnp.float32
     vmem = pl.BlockSpec(memory_space=pltpu.VMEM)
     side = pltpu.VMEM((2, groups, variables, SUB, LANES), f32)
+    field = pltpu.VMEM((groups, variables, rows + 4, SUB, LANES), f32)
     dma = pltpu.SemaphoreType.DMA
     basis, upper = pl.pallas_call(
         functools.partial(kernel, (vectors, variables, rows, n_ax, n_rad)),
@@ -314,10 +340,16 @@
             jax.ShapeDtypeStruct((vectors * cells, LANES), f32),
             jax.ShapeDtypeStruct((vectors, vectors), f32),
         ),
-        in_specs=[vmem, vmem, vmem, vmem, pl.BlockSpec(memory_space=pltpu.SMEM)],
+        in_specs=[pl.BlockSpec(memory_space=pl.ANY)] * 5,
         out_specs=(vmem, vmem),
         scratch_shapes=[
-            pltpu.VMEM((2, groups, variables, rows + 4, SUB, LANES), f32),
+            pltpu.VMEM((vectors * cells, LANES), f32),
+            pltpu.VMEM((rows, LANES), f32),
+            pltpu.VMEM((rows, LANES), f32),
+            pltpu.VMEM((variables, variables, rows, LANES), f32),
+            pltpu.SMEM((variables,), f32),
+            dma((groups + 4,)),
+            field, field,
             pltpu.VMEM((variables, rows, 8 + variables, SUB, LANES), f32),
             side, side, side,
             pltpu.VMEM((variables, rows // 2, LANES, 2 * LANES), jnp.bfloat16),

time: 110 us -> 111 us (level)
    pallas_call x1, Pallas kernels: 103 us -> 104 us  [per_device(): pl.pallas_call(functools.partial(kernel, (vectors, variables, rows, n_ax,...]
where the time goes in v2:
time: 111 us
  Pallas kernels  104 us (94%)
  local copies, waits for them, and re-layouts  5.95 us (5%)
    pallas_call x1, Pallas kernels, per_device(): pl.pallas_call(functools.partial(kernel, (vectors, variables, rows, n_ax,...  104 us
    unnamed x12, local copies, waits for them, and re-layouts  5.95 us

profile of v2, /device:TPU:0, one launch (start us, length us, event | category | flops | bytes accessed | tf_op | source)
XLA Modules:
  0.0 110.7 jit_solution(2823650039655232323)
XLA Ops:
  0.6 0.0 copy-start
  0.6 1.3 %copy-done = f32[32,5,16,128]{3,2,1,0:T(8,128)S(1)} copy-done((f32[32,5,16,128]{3,2,1,0:T(8,128)S(1)}, f32[32,5,16,128]{3,2,1,0:T(8,128)}, u32[]{:S(2)}) %copy-start) | copy-done | bytes 1310744
  1.9 0.0 copy-start.1
  2.0 0.9 copy-done.1
  2.9 0.0 copy-start.2
  2.9 0.7 copy-done.2
  3.6 0.0 copy-start.3
  3.6 0.7 copy-done.3
  4.3 0.0 copy-start.4
  4.3 0.7 copy-done.4
  4.9 104.1 %shard_map.68 = (f32[2560,128]{1,0:T(8,128)S(1)}, f32[32,32]{1,0:T(8,128)S(1)}) custom-call(f32[2560,128]{1,0:T(8,128)S(1)} %bitcast.2, f32[16,128]{1,0:T(8,128)S(1)} %copy-done.2, f32[16,128]{1,0:T(8,128)S(1)} %copy-done.3, f32[5,5,16,128]{3,2,1,0:T(8,128)S(1)} %copy-done.1, f32[5]{0:T(128)S(1)} %copy-done.4), custom_call_target="tpu_custom_call" | custom-call | tf_op jit(solution)/shard_map/pallas_call | solution.py:337
  109.1 1.1 copy.9
  110.1 0.6 copy.10
Async XLA Ops:
  0.6 1.3 %copy-start = (f32[32,5,16,128]{3,2,1,0:T(8,128)S(1)}, f32[32,5,16,128]{3,2,1,0:T(8,128)}, u32[]{:S(2)}) copy-start(f32[32,5,16,128]{3,2,1,0:T(8,128)} %param.5) | copy-start | bytes 3932164
  1.9 0.9 copy-start.1
  2.9 0.7 copy-start.2
  3.6 0.7 copy-start.3
  4.3 0.7 copy-start.4

commit v3 on v2

--- a/solution.py
+++ b/solution.py
@@ -16,9 +16,9 @@
 
 
 def kernel(
-    sizes, f_ref, va_ref, vr_ref, cp_ref, nu_ref, out_ref, r_ref,
+    sizes, f_ref, va_ref, vr_ref, cp_ref, nu_ref, split_out, folded_ref,
     forcing_in, va_in, vr_in, cp_in, nu_in, in_sem,
-    field_0, field_1, coef, packed, from_left, from_right, split, mine, rad_slots, ax_slots,
+    field_0, field_1, coef, packed, from_left, from_right, split, split_sem, mine, rad_slots, ax_slots,
     send_sem, recv_sem, rad_send, rad_recv, ax_send, ax_recv,
 ):
     vectors, variables, rows, n_ax, n_rad = sizes
@@ -220,6 +220,9 @@
 
     lax.fori_loop(0, STEPS, both_halves, 0)
 
+    def leave(v):
+        return pltpu.make_async_copy(split.at[v], split_out.at[v], split_sem.at[v])
+
     def products(v, total):
         for p in range(rows // 2):
             for e in range(2):
@@ -236,6 +239,7 @@
                 both[: 2 * vectors], both, (((1,), (1,)), ((), ())),
                 preferred_element_type=jnp.float32,
             )
+        leave(v).start()
         return total
 
     total = lax.fori_loop(
@@ -275,6 +279,25 @@
     folded = sum_over(
         folded, n_ax, ax, lambda i: (i, rad), ax_slots, ax_send, ax_recv, mine.at[1]
     )
+
+    folded_ref[...] = folded
+    for v in range(variables):
+        leave(v).wait()
+
+
+def finish(sizes, folded_ref, split_in, out_ref, r_ref, split, basis, in_sem, out_sem):
+    vectors, variables, rows, n_ax, n_rad = sizes
+    lane = lax.broadcasted_iota(jnp.int32, (SUB, LANES), 1)
+    sub = lax.broadcasted_iota(jnp.int32, (SUB, LANES), 0)
+    quarter = lane // vectors
+    tile = (SUB, LANES)
+    folded = folded_ref[...]
+
+    def enter(v):
+        return pltpu.make_async_copy(split_in.at[v], split.at[v], in_sem.at[v])
+
+    for v in range(variables):
+        enter(v).start()
 
     blocks = []
     for b in range(vectors // SUB):
@@ -311,16 +334,20 @@
     wide = lax.broadcasted_iota(jnp.int32, (vectors, LANES), 1)
     factors = jnp.where(wide < 2 * vectors, high, inverse - high).astype(jnp.bfloat16)
 
-    def outputs(v, carry):
+    def leave(v):
+        return pltpu.make_async_copy(
+            basis.at[:, v], out_ref.at[:, v], out_sem.at[v]
+        )
+
+    for v in range(variables):
+        enter(v).wait()
         for p in range(rows // 2):
             found = jnp.dot(factors, split[v, p], preferred_element_type=jnp.float32)
             for e in range(2):
-                out_ref[pl.ds(v * rows + 2 * p + e, vectors, stride=cells), :] = found[
-                    :, e * LANES : (e + 1) * LANES
-                ]
-        return carry
-
-    lax.fori_loop(0, variables, outputs, 0)
+                basis[:, v, 2 * p + e, :] = found[:, e * LANES : (e + 1) * LANES]
+        leave(v).start()
+    for v in range(variables):
+        leave(v).wait()
 
 
 def per_device(forcing, vel_axial, vel_radial, coupling, viscosity):
@@ -334,14 +361,16 @@
     side = pltpu.VMEM((2, groups, variables, SUB, LANES), f32)
     field = pltpu.VMEM((groups, variables, rows + 4, SUB, LANES), f32)
     dma = pltpu.SemaphoreType.DMA
-    basis, upper = pl.pallas_call(
-        functools.partial(kernel, (vectors, variables, rows, n_ax, n_rad)),
+    sizes = (vectors, variables, rows, n_ax, n_rad)
+    hbm = pl.BlockSpec(memory_space=pltpu.HBM)
+    split, folded = pl.pallas_call(
+        functools.partial(kernel, sizes),
         out_shape=(
-            jax.ShapeDtypeStruct((vectors * cells, LANES), f32),
-            jax.ShapeDtypeStruct((vectors, vectors), f32),
+            jax.ShapeDtypeStruct((variables, rows // 2, LANES, 2 * LANES), jnp.bfloat16),
+            jax.ShapeDtypeStruct((SUB, LANES), f32),
         ),
-        in_specs=[pl.BlockSpec(memory_space=pl.ANY)] * 5,
-        out_specs=(vmem, vmem),
+        in_specs=[hbm] * 5,
+        out_specs=(hbm, vmem),
         scratch_shapes=[
             pltpu.VMEM((vectors * cells, LANES), f32),
             pltpu.VMEM((rows, LANES), f32),
@@ -353,6 +382,7 @@
             pltpu.VMEM((variables, rows, 8 + variables, SUB, LANES), f32),
             side, side, side,
             pltpu.VMEM((variables, rows // 2, LANES, 2 * LANES), jnp.bfloat16),
+            dma((variables,)),
             pltpu.VMEM((2, SUB, LANES), f32),
             pltpu.VMEM((n_rad, SUB, LANES), f32),
             pltpu.VMEM((n_ax, SUB, LANES), f32),
@@ -360,10 +390,24 @@
             dma((n_rad,)), dma((n_rad,)), dma((n_ax,)), dma((n_ax,)),
         ],
         compiler_params=pltpu.CompilerParams(
-            collective_id=0, has_side_effects=True, vmem_limit_bytes=48 * 2**20
+            collective_id=0, has_side_effects=True, vmem_limit_bytes=64 * 2**20
         ),
     )(forcing.reshape(vectors * cells, LANES), vel_axial, vel_radial, coupling, viscosity)
-    return basis.reshape(forcing.shape), upper
+    return pl.pallas_call(
+        functools.partial(finish, sizes),
+        out_shape=(
+            jax.ShapeDtypeStruct(forcing.shape, f32),
+            jax.ShapeDtypeStruct((vectors, vectors), f32),
+        ),
+        in_specs=[vmem, hbm],
+        out_specs=(hbm, vmem),
+        scratch_shapes=[
+            pltpu.VMEM(split.shape, split.dtype),
+            pltpu.VMEM(forcing.shape, f32),
+            dma((variables,)), dma((variables,)),
+        ],
+        compiler_params=pltpu.CompilerParams(vmem_limit_bytes=64 * 2**20),
+    )(folded, split)
 
 
 def solution(mesh):

time: 111 us -> 107 us (0.964)
  local copies, waits for them, and re-layouts: 5.95 us -> 0 us
  Pallas kernels: 104 us -> 106 us
    unnamed x12 -> x0, local copies, waits for them, and re-layouts: 5.95 us -> none
    pallas_call x1 -> x2, Pallas kernels: 104 us -> 106 us  [the longest x1 98.6 us: per_device(): pl.pallas_call(functools.partial(kernel, sizes), out_shape=(jax.ShapeDtyp...]
where the time goes in v3:
time: 107 us
  Pallas kernels  106 us (99%)
    pallas_call x1, Pallas kernels, per_device(): pl.pallas_call(functools.partial(kernel, sizes), out_shape=(jax.ShapeDtyp...  98.6 us
    pallas_call x1, Pallas kernels, per_device(): pl.pallas_call(functools.partial(finish, sizes), out_shape=(jax.ShapeDtyp...  7.59 us

profile of v3, /device:TPU:0, one launch (start us, length us, event | category | flops | bytes accessed | tf_op | source)
XLA Modules:
  0.0 106.8 jit_solution(10865459930030929634)
XLA Ops:
  0.6 98.6 %shard_map.68 = (bf16[5,8,128,256]{3,2,1,0:T(8,128)(2,1)}, f32[8,128]{1,0:T(8,128)}) custom-call(f32[2560,128]{1,0:T(8,128)} %bitcast.1, f32[16,128]{1,0:T(8,128)} %va_ref.1, f32[16,128]{1,0:T(8,128)} %vr_ref.1, f32[5,5,16,128]{3,2,1,0:T(8,128)} %cp_ref.1, f32[5]{0:T(128)} %nu_ref.1), custom_call_target="tpu_custom_call" | custom-call | tf_op jit(solution)/shard_map/pallas_call | solution.py:366
  99.2 7.6 %shard_map.69 = (f32[32,5,16,128]{3,2,1,0:T(8,128)}, f32[32,32]{1,0:T(8,128)}) custom-call(f32[8,128]{1,0:T(8,128)} %get-tuple-element.4.folded_ref, bf16[5,8,128,256]{3,2,1,0:T(8,128)(2,1)} %get-tuple-element.5.split_in), custom_call_target="tpu_custom_call" | custom-call | tf_op jit(solution)/shard_map/pallas_call | solution.py:396

commit v4 on v3

--- a/solution.py
+++ b/solution.py
@@ -199,8 +199,15 @@
             def one_group(g, inner):
                 for d in range(4):
                     wait_recv(src, g, d)
-                for d in range(4):
-                    wait_send(src, g, d)
+                if src == 1:
+                    for d in range(4):
+                        wait_send(0, g, d)
+                else:
+                    @pl.when(step > 0)
+                    def _():
+                        for d in range(4):
+                            wait_send(1, g, d)
+
 
                 def send(directions):
                     @pl.when(more)
@@ -219,6 +226,13 @@
         return carry
 
     lax.fori_loop(0, STEPS, both_halves, 0)
+
+    def drain(g, carry):
+        for d in range(4):
+            wait_send(1, g, d)
+        return carry
+
+    lax.fori_loop(0, groups, drain, 0)
 
     def leave(v):
         return pltpu.make_async_copy(split.at[v], split_out.at[v], split_sem.at[v])
@@ -304,19 +318,30 @@
         part = folded if b == 0 else pltpu.roll(folded, LANES - vectors * b, 1)
         unit = jnp.where(lane - vectors == sub + SUB * b, 1.0, 0.0)
         blocks.append(jnp.where(lane < vectors, part, unit))
-    for j in range(vectors):
+    for j in range(0, vectors, 2):
         jb, js = j // SUB, j % SUB
-        row = jnp.broadcast_to(blocks[jb][js : js + 1, :], tile)
-        columns = {
-            b: jnp.broadcast_to(blocks[b][:, j : j + 1], tile) for b in range(jb, len(blocks))
-        }
-        pivot = jnp.broadcast_to(columns[jb][js : js + 1, :], tile)
-        scaled = row * (1.0 / pivot)
-        for b in range(jb, len(blocks)):
-            change = columns[b] * scaled
+        below = range(jb, len(blocks))
+        first = jnp.broadcast_to(blocks[jb][js : js + 1, :], tile)
+        second = jnp.broadcast_to(blocks[jb][js + 1 : js + 2, :], tile)
+        column = {b: jnp.broadcast_to(blocks[b][:, j : j + 1], tile) for b in below}
+        other = {b: jnp.broadcast_to(blocks[b][:, j + 1 : j + 2], tile) for b in below}
+
+        def entry(columns, i):
+            return jnp.broadcast_to(columns[jb][i : i + 1, :], tile)
+
+        over = 1.0 / entry(column, js)
+        ratio = entry(column, js + 1) * over
+        across = entry(other, js) * over
+        last = 1.0 / (entry(other, js + 1) - ratio * entry(other, js))
+        first_scaled = first * over
+        second_scaled = (second - ratio * first) * last
+        for b in below:
+            change = column[b] * first_scaled
+            more = (other[b] - column[b] * across) * second_scaled
             if b == jb:
                 change = jnp.where(sub > js, change, 0.0)
-            blocks[b] = blocks[b] - change
+                more = jnp.where(sub > js + 1, more, 0.0)
+            blocks[b] = blocks[b] - change - more
     lefts, rights = [], []
     for b, block in enumerate(blocks):
         diagonal = jnp.sum(

time: 107 us -> 106 us (level)
    pallas_call x1, Pallas kernels: 7.59 us -> 6.39 us  [per_device(): pl.pallas_call(functools.partial(finish, sizes), out_shape=(jax.ShapeDtyp...]
where the time goes in v4:
time: 106 us
  Pallas kernels  105 us (99%)
    pallas_call x1, Pallas kernels, per_device(): pl.pallas_call(functools.partial(kernel, sizes), out_shape=(jax.ShapeDtyp...  98.9 us
    pallas_call x1, Pallas kernels, per_device(): pl.pallas_call(functools.partial(finish, sizes), out_shape=(jax.ShapeDtyp...  6.39 us

profile of v4, /device:TPU:0, one launch (start us, length us, event | category | flops | bytes accessed | tf_op | source)
XLA Modules:
  0.0 105.9 jit_solution(9462385441581799825)
XLA Ops:
  0.6 98.9 %shard_map.68 = (bf16[5,8,128,256]{3,2,1,0:T(8,128)(2,1)}, f32[8,128]{1,0:T(8,128)}) custom-call(f32[2560,128]{1,0:T(8,128)} %bitcast.1, f32[16,128]{1,0:T(8,128)} %va_ref.1, f32[16,128]{1,0:T(8,128)} %vr_ref.1, f32[5,5,16,128]{3,2,1,0:T(8,128)} %cp_ref.1, f32[5]{0:T(128)} %nu_ref.1), custom_call_target="tpu_custom_call" | custom-call | tf_op jit(solution)/shard_map/pallas_call | solution.py:391
  99.5 6.4 %shard_map.69 = (f32[32,5,16,128]{3,2,1,0:T(8,128)}, f32[32,32]{1,0:T(8,128)}) custom-call(f32[8,128]{1,0:T(8,128)} %get-tuple-element.4.folded_ref, bf16[5,8,128,256]{3,2,1,0:T(8,128)(2,1)} %get-tuple-element.5.split_in), custom_call_target="tpu_custom_call" | custom-call | tf_op jit(solution)/shard_map/pallas_call | solution.py:421

commit v5 on v4

--- a/solution.py
+++ b/solution.py
@@ -17,22 +17,27 @@
 
 def kernel(
     sizes, f_ref, va_ref, vr_ref, cp_ref, nu_ref, split_out, folded_ref,
-    forcing_in, va_in, vr_in, cp_in, nu_in, in_sem,
+    forcing_in, va_in, vr_in, cp_in, nu_in, in_sem, swap_send, swap_recv,
+    response, back_own, back_send, back_recv,
     field_0, field_1, coef, packed, from_left, from_right, split, split_sem, mine, rad_slots, ax_slots,
     send_sem, recv_sem, rad_send, rad_recv, ax_send, ax_recv,
 ):
-    vectors, variables, rows, n_ax, n_rad = sizes
-    groups = vectors // SUB
-    cells = variables * rows
+    vectors, variables, own_rows, n_ax, n_rad = sizes
+    rows = 2 * own_rows
+    groups = vectors // SUB // 2
+    cells = variables * own_rows
+    pieces_a_side = rows * 8 // LANES
     fields = (field_0, field_1)
     ax = lax.axis_index("ax")
     rad = lax.axis_index("rad")
-    ax_before = lax.rem(ax + n_ax - 1, n_ax)
-    ax_after = lax.rem(ax + 1, n_ax)
+    ax_before = lax.rem(ax + n_ax - 2, n_ax)
+    ax_after = lax.rem(ax + 2, n_ax)
+    half_index = lax.rem(ax, 2)
+    partner = ax + 1 - 2 * half_index
     rad_before = lax.rem(rad + n_rad - 1, n_rad)
     rad_after = lax.rem(rad + 1, n_rad)
-    sends = (ax > 0, ax < n_ax - 1, rad > 0, rad < n_rad - 1)
-    takes = (ax < n_ax - 1, ax > 0, rad < n_rad - 1, rad > 0)
+    sends = (ax > 1, ax < n_ax - 2, rad > 0, rad < n_rad - 1)
+    takes = (ax < n_ax - 2, ax > 1, rad < n_rad - 1, rad > 0)
     lane = lax.broadcasted_iota(jnp.int32, (SUB, LANES), 1)
     sub = lax.broadcasted_iota(jnp.int32, (SUB, LANES), 0)
     slot = lane // 8
@@ -73,23 +78,32 @@
             link(buf, g, d).wait_recv()
 
     part = SUB * cells
-    pieces = [
-        pltpu.make_async_copy(
-            f_ref.at[pl.ds(g * part, part)], forcing_in.at[pl.ds(g * part, part)], in_sem.at[g]
-        )
-        for g in range(groups)
-    ]
-    others = [
-        pltpu.make_async_copy(source, target, in_sem.at[groups + i])
-        for i, (source, target) in enumerate(
-            ((va_ref, va_in), (vr_ref, vr_in), (cp_ref, cp_in), (nu_ref, nu_in))
-        )
-    ]
-    for copy in pieces + others:
+
+    def enter(i):
+        if i < groups:
+            span = pl.ds((half_index * groups + i) * part, part)
+            return f_ref.at[span], forcing_in.at[half_index, pl.ds(i * part, part)]
+        source, target = ((va_ref, va_in), (vr_ref, vr_in), (cp_ref, cp_in))[i - groups]
+        return source, target.at[half_index]
+
+    def swap(i):
+        source, target = enter(i)
+        if i < groups:
+            source = f_ref.at[pl.ds(((1 - half_index) * groups + i) * part, part)]
+        return pltpu.make_async_remote_copy(
+            src_ref=source, dst_ref=target,
+            send_sem=swap_send.at[i], recv_sem=swap_recv.at[i],
+            device_id=(partner, rad), device_id_type=MESH,
+        )
+
+    own = [pltpu.make_async_copy(*enter(i), in_sem.at[i]) for i in range(groups + 3)]
+    own.append(pltpu.make_async_copy(nu_ref, nu_in, in_sem.at[groups + 3]))
+    swaps = [swap(i) for i in range(groups + 3)]
+    for copy in own:
         copy.start()
 
     zero_rows = jnp.zeros((variables, 2, SUB, LANES), jnp.float32)
-    zero_side = jnp.zeros((variables, SUB, LANES), jnp.float32)
+    zero_side = jnp.zeros((variables, pieces_a_side, SUB, LANES), jnp.float32)
     for buf in range(2):
         for g in range(groups):
             fields[buf][g, :, 0:2] = zero_rows
@@ -107,40 +121,56 @@
             barrier, inc=1, device_id=(ax, lax.rem(rad + step, n_rad)), device_id_type=MESH
         )
 
-    for g in range(groups):
-        pieces[g].wait()
-        for v in range(variables):
-            pack = jnp.zeros(tile, jnp.float32)
-            for a in range(rows):
-                value = forcing_in[pl.ds(g * part + v * rows + a, SUB, stride=cells), :]
-                field_0[g, v, a + 2] = value
-                pack = jnp.where(slot == a, pltpu.roll(value, 2 + 8 * a, 1), pack)
-            packed[0, g, v] = pack
-        if g == 0:
-            pl.semaphore_wait(barrier, n_ax + n_rad - 2)
-        for d in range(4):
-            start(0, g, d)
-    for copy in others:
-        copy.wait()
-
-    def prepare(a, carry):
-        vel_a = jnp.broadcast_to(va_in[pl.ds(a, 1), :], tile) * (time_step / 12.0)
-        vel_r = jnp.broadcast_to(vr_in[pl.ds(a, 1), :], tile) * (time_step / 12.0)
+    pl.semaphore_wait(barrier, n_ax + n_rad - 2)
+    order = list(range(groups, groups + 3)) + list(range(groups))
+    for i in order:
+        swaps[i].start()
+    own[groups + 3].wait()
+    for i in range(groups, groups + 3):
+        own[i].wait()
+        swaps[i].wait_recv()
+
+    def prepare(h, a, carry):
+        vel_a = jnp.broadcast_to(va_in[h, pl.ds(a, 1), :], tile) * (time_step / 12.0)
+        vel_r = jnp.broadcast_to(vr_in[h, pl.ds(a, 1), :], tile) * (time_step / 12.0)
         for v in range(variables):
             nu = jnp.full(tile, nu_in[v], jnp.float32) * (time_step / 12.0)
             terms = []
             for vel in (vel_a, vel_r):
                 terms += [16.0 * nu - 8.0 * vel, 16.0 * nu + 8.0 * vel, vel - nu, -vel - nu]
             for w in range(variables):
-                term = time_step * jnp.broadcast_to(cp_in[v, w, pl.ds(a, 1), :], tile)
+                term = time_step * jnp.broadcast_to(cp_in[h, v, w, pl.ds(a, 1), :], tile)
                 if w == v:
                     term = term + (1.0 - 60.0 * nu)
                 terms.append(term)
             for t, term in enumerate(terms):
-                coef[v, a, t] = term
+                coef[v, h * own_rows + a, t] = term
         return carry
 
-    lax.fori_loop(0, rows, prepare, 0)
+    for h in range(2):
+        lax.fori_loop(0, own_rows, functools.partial(prepare, h), 0)
+
+    for g in range(groups):
+        own[g].wait()
+        swaps[g].wait_recv()
+
+        def bring(v, carry):
+            packs = [jnp.zeros(tile, jnp.float32) for _ in range(pieces_a_side)]
+            for a in range(rows):
+                start_row = g * part + v * own_rows + a % own_rows
+                value = forcing_in[a // own_rows, pl.ds(start_row, SUB, stride=cells), :]
+                field_0[g, v, a + 2] = value
+                p, at = a * 8 // LANES, a % (LANES // 8)
+                packs[p] = jnp.where(slot == at, pltpu.roll(value, 2 + 8 * at, 1), packs[p])
+            for p, pack in enumerate(packs):
+                packed[0, g, v, p] = pack
+            return carry
+
+        lax.fori_loop(0, variables, bring, 0)
+        for d in range(4):
+            start(0, g, d)
+    for copy in swaps:
+        copy.wait_send()
 
     def advance(src, g, start_axial):
         dst = 1 - src
@@ -153,16 +183,23 @@
                 later[g, v, a + 2] = value
 
         sides = [
-            jnp.where(lane % 8 < 2, from_left[src, g, v], from_right[src, g, v])
+            [
+                jnp.where(lane % 8 < 2, from_left[src, g, v, p], from_right[src, g, v, p])
+                for p in range(pieces_a_side)
+            ]
             for v in range(variables)
         ]
-        packs = [jnp.zeros(tile, jnp.float32) for _ in range(variables)]
+        packs = [
+            [jnp.zeros(tile, jnp.float32) for _ in range(pieces_a_side)]
+            for _ in range(variables)
+        ]
         order = [0, 1, rows - 2, rows - 1] + list(range(2, rows - 2))
         for count, a in enumerate(order):
+            p, at = a * 8 // LANES, a % (LANES // 8)
             centre = [now[g, v, a + 2] for v in range(variables)]
             for v in range(variables):
                 x = centre[v]
-                side = pltpu.roll(sides[v], (2 * LANES - 2 - 8 * a) % LANES, 1)
+                side = pltpu.roll(sides[v][p], (2 * LANES - 2 - 8 * at) % LANES, 1)
                 near = [
                     now[g, v, a + 3],
                     now[g, v, a + 1],
@@ -183,14 +220,31 @@
                 if src == 1:
                     new = 0.5 * (later[g, v, a + 2] + new)
                 held.append((v, a, new))
-                packs[v] = jnp.where(slot == a, pltpu.roll(new, 2 + 8 * a, 1), packs[v])
+                packs[v][p] = jnp.where(
+                    slot == at, pltpu.roll(new, 2 + 8 * at, 1), packs[v][p]
+                )
             if count == 3:
                 store(0)
                 start_axial()
             store(2 * variables)
         store(0)
         for v in range(variables):
-            packed[dst, g, v] = packs[v]
+            for p in range(pieces_a_side):
+                packed[dst, g, v, p] = packs[v][p]
+
+    def back(g):
+        return pltpu.make_async_remote_copy(
+            src_ref=field_0.at[g, :, pl.ds(2 + (1 - half_index) * own_rows, own_rows)],
+            dst_ref=response.at[half_index * groups + g],
+            send_sem=back_send.at[g], recv_sem=back_recv.at[g],
+            device_id=(partner, rad), device_id_type=MESH,
+        )
+
+    def keep(g):
+        return pltpu.make_async_copy(
+            field_0.at[g, :, pl.ds(2 + half_index * own_rows, own_rows)],
+            response.at[half_index * groups + g], back_own.at[g],
+        )
 
     def both_halves(step, carry):
         def half(src):
@@ -217,6 +271,11 @@
 
                 advance(src, g, lambda: send((0, 1)))
                 send((2, 3))
+                if src == 1:
+                    @pl.when(step == STEPS - 1)
+                    def _():
+                        back(g).start()
+                        keep(g).start()
                 return inner
 
             lax.fori_loop(0, groups, one_group, 0)
@@ -233,15 +292,19 @@
         return carry
 
     lax.fori_loop(0, groups, drain, 0)
+    for g in range(groups):
+        keep(g).wait()
+        back(g).wait_recv()
+        back(g).wait_send()
 
     def leave(v):
         return pltpu.make_async_copy(split.at[v], split_out.at[v], split_sem.at[v])
 
     def products(v, total):
-        for p in range(rows // 2):
+        for p in range(own_rows // 2):
             for e in range(2):
                 x = jnp.concatenate(
-                    [field_0[g, v, 2 * p + e + 2] for g in range(groups)], axis=0
+                    [response[g, v, 2 * p + e] for g in range(2 * groups)], axis=0
                 )
                 high = x.astype(jnp.bfloat16)
                 low = (x - high.astype(jnp.float32)).astype(jnp.bfloat16)
@@ -379,12 +442,14 @@
     vectors, variables, rows, columns = forcing.shape
     n_ax, n_rad = lax.axis_size("ax"), lax.axis_size("rad")
     groups = vectors // SUB
+    half = groups // 2
     cells = variables * rows
+    assert lax.axis_size("ax") % 2 == 0
     assert columns == LANES and rows * 8 == LANES and vectors * 4 == LANES
     f32 = jnp.float32
     vmem = pl.BlockSpec(memory_space=pltpu.VMEM)
-    side = pltpu.VMEM((2, groups, variables, SUB, LANES), f32)
-    field = pltpu.VMEM((groups, variables, rows + 4, SUB, LANES), f32)
+    side = pltpu.VMEM((2, half, variables, 2 * rows * 8 // LANES, SUB, LANES), f32)
+    field = pltpu.VMEM((half, variables, 2 * rows + 4, SUB, LANES), f32)
     dma = pltpu.SemaphoreType.DMA
     sizes = (vectors, variables, rows, n_ax, n_rad)
     hbm = pl.BlockSpec(memory_space=pltpu.HBM)
@@ -397,21 +462,23 @@
         in_specs=[hbm] * 5,
         out_specs=(hbm, vmem),
         scratch_shapes=[
-            pltpu.VMEM((vectors * cells, LANES), f32),
-            pltpu.VMEM((rows, LANES), f32),
-            pltpu.VMEM((rows, LANES), f32),
-            pltpu.VMEM((variables, variables, rows, LANES), f32),
+            pltpu.VMEM((2, half * SUB * cells, LANES), f32),
+            pltpu.VMEM((2, rows, LANES), f32),
+            pltpu.VMEM((2, rows, LANES), f32),
+            pltpu.VMEM((2, variables, variables, rows, LANES), f32),
             pltpu.SMEM((variables,), f32),
-            dma((groups + 4,)),
+            dma((half + 4,)), dma((half + 3,)), dma((half + 3,)),
+            pltpu.VMEM((groups, variables, rows, SUB, LANES), f32),
+            dma((half,)), dma((half,)), dma((half,)),
             field, field,
-            pltpu.VMEM((variables, rows, 8 + variables, SUB, LANES), f32),
+            pltpu.VMEM((variables, 2 * rows, 8 + variables, SUB, LANES), f32),
             side, side, side,
             pltpu.VMEM((variables, rows // 2, LANES, 2 * LANES), jnp.bfloat16),
             dma((variables,)),
             pltpu.VMEM((2, SUB, LANES), f32),
             pltpu.VMEM((n_rad, SUB, LANES), f32),
             pltpu.VMEM((n_ax, SUB, LANES), f32),
-            dma((2, groups, 4)), dma((2, groups, 4)),
+            dma((2, half, 4)), dma((2, half, 4)),
             dma((n_rad,)), dma((n_rad,)), dma((n_ax,)), dma((n_ax,)),
         ],
         compiler_params=pltpu.CompilerParams(

time: 106 us -> 165 us (1.56)
  Pallas kernels: 105 us -> 164 us
    pallas_call x1, Pallas kernels: 98.9 us -> 158 us  [per_device(): pl.pallas_call(functools.partial(kernel, sizes), out_shape=(jax.ShapeDtyp...]
where the time goes in v5:
time: 165 us
  Pallas kernels  164 us (99%)
    pallas_call x1, Pallas kernels, per_device(): pl.pallas_call(functools.partial(kernel, sizes), out_shape=(jax.ShapeDtyp...  158 us
    pallas_call x1, Pallas kernels, per_device(): pl.pallas_call(functools.partial(finish, sizes), out_shape=(jax.ShapeDtyp...  6.39 us

profile of v5, /device:TPU:0, one launch (start us, length us, event | category | flops | bytes accessed | tf_op | source)
XLA Modules:
  0.0 164.6 jit_solution(15345806835010232806)
XLA Ops:
  0.6 157.6 %shard_map.68 = (bf16[5,8,128,256]{3,2,1,0:T(8,128)(2,1)}, f32[8,128]{1,0:T(8,128)}) custom-call(f32[2560,128]{1,0:T(8,128)} %bitcast.1, f32[16,128]{1,0:T(8,128)} %va_ref.1, f32[16,128]{1,0:T(8,128)} %vr_ref.1, f32[5,5,16,128]{3,2,1,0:T(8,128)} %cp_ref.1, f32[5]{0:T(128)} %nu_ref.1), custom_call_target="tpu_custom_call" | custom-call | tf_op jit(solution)/shard_map/pallas_call | solution.py:456
  158.2 6.4 %shard_map.69 = (f32[32,5,16,128]{3,2,1,0:T(8,128)}, f32[32,32]{1,0:T(8,128)}) custom-call(f32[8,128]{1,0:T(8,128)} %get-tuple-element.4.folded_ref, bf16[5,8,128,256]{3,2,1,0:T(8,128)(2,1)} %get-tuple-element.5.split_in), custom_call_target="tpu_custom_call" | custom-call | tf_op jit(solution)/shard_map/pallas_call | solution.py:488

commit v6 on v4

--- a/solution.py
+++ b/solution.py
@@ -90,12 +90,15 @@
 
     zero_rows = jnp.zeros((variables, 2, SUB, LANES), jnp.float32)
     zero_side = jnp.zeros((variables, SUB, LANES), jnp.float32)
-    for buf in range(2):
-        for g in range(groups):
+    def clear(g, carry):
+        for buf in range(2):
             fields[buf][g, :, 0:2] = zero_rows
             fields[buf][g, :, rows + 2 : rows + 4] = zero_rows
             from_left[buf, g] = zero_side
             from_right[buf, g] = zero_side
+        return carry
+
+    lax.fori_loop(0, groups, clear, 0)
 
     barrier = pltpu.get_barrier_semaphore()
     for step in range(1, n_ax):
@@ -109,13 +112,16 @@
 
     for g in range(groups):
         pieces[g].wait()
-        for v in range(variables):
+        def bring(v, carry):
             pack = jnp.zeros(tile, jnp.float32)
             for a in range(rows):
                 value = forcing_in[pl.ds(g * part + v * rows + a, SUB, stride=cells), :]
                 field_0[g, v, a + 2] = value
                 pack = jnp.where(slot == a, pltpu.roll(value, 2 + 8 * a, 1), pack)
             packed[0, g, v] = pack
+            return carry
+
+        lax.fori_loop(0, variables, bring, 0)
         if g == 0:
             pl.semaphore_wait(barrier, n_ax + n_rad - 2)
         for d in range(4):
@@ -142,53 +148,57 @@
 
     lax.fori_loop(0, rows, prepare, 0)
 
-    def advance(src, g, start_axial):
+    block = 4
+
+    def advance(src, g):
         dst = 1 - src
         now, later = fields[src], fields[dst]
-        held = []
-
-        def store(keep):
-            while len(held) > keep:
-                v, a, value = held.pop(0)
-                later[g, v, a + 2] = value
+
+        def turn(i, carry):
+            sides, packs = carry
+            base = block * i
+            packs = [pltpu.roll(pack, LANES - 8 * block, 1) for pack in packs]
+            done = []
+            for k in range(block):
+                a = base + k
+                at = rows - block + k
+                centre = [now[g, v, a + 2] for v in range(variables)]
+                for v in range(variables):
+                    x = centre[v]
+                    side = pltpu.roll(sides[v], LANES - 2 - 8 * k, 1)
+                    near = [
+                        now[g, v, a + 3],
+                        now[g, v, a + 1],
+                        now[g, v, a + 4],
+                        now[g, v, a],
+                        pltpu.roll(jnp.where(lane == 0, side, x), LANES - 1, 1),
+                        pltpu.roll(jnp.where(lane == LANES - 1, side, x), 1, 1),
+                        pltpu.roll(jnp.where(lane < 2, side, x), LANES - 2, 1),
+                        pltpu.roll(jnp.where(lane >= LANES - 2, side, x), 2, 1),
+                    ]
+                    parts = [coef[v, a, t] * q for t, q in enumerate(near + centre)]
+                    while len(parts) > 1:
+                        parts = [
+                            parts[j] + parts[j + 1] if j + 1 < len(parts) else parts[j]
+                            for j in range(0, len(parts), 2)
+                        ]
+                    new = parts[0]
+                    if src == 1:
+                        new = 0.5 * (later[g, v, a + 2] + new)
+                    done.append((v, a, new))
+                    packs[v] = jnp.where(
+                        slot == at, pltpu.roll(new, (2 + 8 * at) % LANES, 1), packs[v]
+                    )
+            for v, a, new in done:
+                later[g, v, a + 2] = new
+            return [pltpu.roll(side, LANES - 8 * block, 1) for side in sides], packs
 
         sides = [
             jnp.where(lane % 8 < 2, from_left[src, g, v], from_right[src, g, v])
             for v in range(variables)
         ]
         packs = [jnp.zeros(tile, jnp.float32) for _ in range(variables)]
-        order = [0, 1, rows - 2, rows - 1] + list(range(2, rows - 2))
-        for count, a in enumerate(order):
-            centre = [now[g, v, a + 2] for v in range(variables)]
-            for v in range(variables):
-                x = centre[v]
-                side = pltpu.roll(sides[v], (2 * LANES - 2 - 8 * a) % LANES, 1)
-                near = [
-                    now[g, v, a + 3],
-                    now[g, v, a + 1],
-                    now[g, v, a + 4],
-                    now[g, v, a],
-                    pltpu.roll(jnp.where(lane == 0, side, x), LANES - 1, 1),
-                    pltpu.roll(jnp.where(lane == LANES - 1, side, x), 1, 1),
-                    pltpu.roll(jnp.where(lane < 2, side, x), LANES - 2, 1),
-                    pltpu.roll(jnp.where(lane >= LANES - 2, side, x), 2, 1),
-                ]
-                parts = [coef[v, a, t] * q for t, q in enumerate(near + centre)]
-                while len(parts) > 1:
-                    parts = [
-                        parts[i] + parts[i + 1] if i + 1 < len(parts) else parts[i]
-                        for i in range(0, len(parts), 2)
-                    ]
-                new = parts[0]
-                if src == 1:
-                    new = 0.5 * (later[g, v, a + 2] + new)
-                held.append((v, a, new))
-                packs[v] = jnp.where(slot == a, pltpu.roll(new, 2 + 8 * a, 1), packs[v])
-            if count == 3:
-                store(0)
-                start_axial()
-            store(2 * variables)
-        store(0)
+        _, packs = lax.fori_loop(0, rows // block, turn, (sides, packs))
         for v in range(variables):
             packed[dst, g, v] = packs[v]
 
@@ -215,8 +225,8 @@
                         for d in directions:
                             start(1 - src, g, d)
 
-                advance(src, g, lambda: send((0, 1)))
-                send((2, 3))
+                advance(src, g)
+                send((2, 3, 0, 1))
                 return inner
 
             lax.fori_loop(0, groups, one_group, 0)
@@ -364,13 +374,16 @@
             basis.at[:, v], out_ref.at[:, v], out_sem.at[v]
         )
 
-    for v in range(variables):
+    def outputs(v, carry):
         enter(v).wait()
         for p in range(rows // 2):
             found = jnp.dot(factors, split[v, p], preferred_element_type=jnp.float32)
             for e in range(2):
                 basis[:, v, 2 * p + e, :] = found[:, e * LANES : (e + 1) * LANES]
         leave(v).start()
+        return carry
+
+    lax.fori_loop(0, variables, outputs, 0)
     for v in range(variables):
         leave(v).wait()
 

time: 106 us -> 70 us (0.66)
  Pallas kernels: 105 us -> 69.1 us
    pallas_call x1, Pallas kernels: 98.9 us -> 62.7 us  [per_device(): pl.pallas_call(functools.partial(kernel, sizes), out_shape=(jax.ShapeDtyp...]
where the time goes in v6:
time: 70 us; the launch traced here: 69.8 us
  Pallas kernels  69.1 us (99%)
    pallas_call x1, Pallas kernels, per_device(): pl.pallas_call(functools.partial(kernel, sizes), out_shape=(jax.ShapeDtyp...  62.7 us
    pallas_call x1, Pallas kernels, per_device(): pl.pallas_call(functools.partial(finish, sizes), out_shape=(jax.ShapeDtyp...  6.4 us

profile of v6, /device:TPU:0, one launch (start us, length us, event | category | flops | bytes accessed | tf_op | source)
XLA Modules:
  0.0 69.8 jit_solution(9730592956403352374)
XLA Ops:
  0.6 62.7 %shard_map.68 = (bf16[5,8,128,256]{3,2,1,0:T(8,128)(2,1)}, f32[8,128]{1,0:T(8,128)}) custom-call(f32[2560,128]{1,0:T(8,128)} %bitcast.1, f32[16,128]{1,0:T(8,128)} %va_ref.1, f32[16,128]{1,0:T(8,128)} %vr_ref.1, f32[5,5,16,128]{3,2,1,0:T(8,128)} %cp_ref.1, f32[5]{0:T(128)} %nu_ref.1), custom_call_target="tpu_custom_call" | custom-call | tf_op jit(solution)/shard_map/pallas_call | solution.py:404
  63.4 6.4 %shard_map.69 = (f32[32,5,16,128]{3,2,1,0:T(8,128)}, f32[32,32]{1,0:T(8,128)}) custom-call(f32[8,128]{1,0:T(8,128)} %get-tuple-element.4.folded_ref, bf16[5,8,128,256]{3,2,1,0:T(8,128)(2,1)} %get-tuple-element.5.split_in), custom_call_target="tpu_custom_call" | custom-call | tf_op jit(solution)/shard_map/pallas_call | solution.py:434

commit v7 on v6

--- a/solution.py
+++ b/solution.py
@@ -149,14 +149,15 @@
     lax.fori_loop(0, rows, prepare, 0)
 
     block = 4
-
-    def advance(src, g):
+    turns = rows // block
+
+    def advance(src, g, start_axial):
         dst = 1 - src
         now, later = fields[src], fields[dst]
 
         def turn(i, carry):
             sides, packs = carry
-            base = block * i
+            base = block * ((i + turns - 1) % turns)
             packs = [pltpu.roll(pack, LANES - 8 * block, 1) for pack in packs]
             done = []
             for k in range(block):
@@ -191,16 +192,24 @@
                     )
             for v, a, new in done:
                 later[g, v, a + 2] = new
+
+            @pl.when(i == 1)
+            def _():
+                start_axial()
+
             return [pltpu.roll(side, LANES - 8 * block, 1) for side in sides], packs
 
         sides = [
-            jnp.where(lane % 8 < 2, from_left[src, g, v], from_right[src, g, v])
+            pltpu.roll(
+                jnp.where(lane % 8 < 2, from_left[src, g, v], from_right[src, g, v]),
+                8 * block, 1,
+            )
             for v in range(variables)
         ]
         packs = [jnp.zeros(tile, jnp.float32) for _ in range(variables)]
-        _, packs = lax.fori_loop(0, rows // block, turn, (sides, packs))
+        _, packs = lax.fori_loop(0, turns, turn, (sides, packs))
         for v in range(variables):
-            packed[dst, g, v] = packs[v]
+            packed[dst, g, v] = pltpu.roll(packs[v], LANES - 8 * block, 1)
 
     def both_halves(step, carry):
         def half(src):
@@ -225,8 +234,8 @@
                         for d in directions:
                             start(1 - src, g, d)
 
-                advance(src, g)
-                send((2, 3, 0, 1))
+                advance(src, g, lambda: send((0, 1)))
+                send((2, 3))
                 return inner
 
             lax.fori_loop(0, groups, one_group, 0)
@@ -328,30 +337,42 @@
         part = folded if b == 0 else pltpu.roll(folded, LANES - vectors * b, 1)
         unit = jnp.where(lane - vectors == sub + SUB * b, 1.0, 0.0)
         blocks.append(jnp.where(lane < vectors, part, unit))
-    for j in range(0, vectors, 2):
-        jb, js = j // SUB, j % SUB
-        below = range(jb, len(blocks))
-        first = jnp.broadcast_to(blocks[jb][js : js + 1, :], tile)
-        second = jnp.broadcast_to(blocks[jb][js + 1 : js + 2, :], tile)
-        column = {b: jnp.broadcast_to(blocks[b][:, j : j + 1], tile) for b in below}
-        other = {b: jnp.broadcast_to(blocks[b][:, j + 1 : j + 2], tile) for b in below}
-
-        def entry(columns, i):
-            return jnp.broadcast_to(columns[jb][i : i + 1, :], tile)
-
-        over = 1.0 / entry(column, js)
-        ratio = entry(column, js + 1) * over
-        across = entry(other, js) * over
-        last = 1.0 / (entry(other, js + 1) - ratio * entry(other, js))
-        first_scaled = first * over
-        second_scaled = (second - ratio * first) * last
-        for b in below:
-            change = column[b] * first_scaled
-            more = (other[b] - column[b] * across) * second_scaled
-            if b == jb:
-                change = jnp.where(sub > js, change, 0.0)
-                more = jnp.where(sub > js + 1, more, 0.0)
-            blocks[b] = blocks[b] - change - more
+    count = len(blocks)
+
+    def eight_rows(i, blocks):
+        blocks = list(blocks)
+        for js in range(0, SUB, 2):
+            jb, j = 0, js
+            below = range(len(blocks))
+            first = jnp.broadcast_to(blocks[jb][js : js + 1, :], tile)
+            second = jnp.broadcast_to(blocks[jb][js + 1 : js + 2, :], tile)
+            column = {b: jnp.broadcast_to(blocks[b][:, j : j + 1], tile) for b in below}
+            other = {b: jnp.broadcast_to(blocks[b][:, j + 1 : j + 2], tile) for b in below}
+
+            def entry(columns, i):
+                return jnp.broadcast_to(columns[jb][i : i + 1, :], tile)
+
+            over = 1.0 / entry(column, js)
+            ratio = entry(column, js + 1) * over
+            across = entry(other, js) * over
+            last = 1.0 / (entry(other, js + 1) - ratio * entry(other, js))
+            first_scaled = first * over
+            second_scaled = (second - ratio * first) * last
+            for b in below:
+                change = column[b] * first_scaled
+                more = (other[b] - column[b] * across) * second_scaled
+                if b == jb:
+                    change = jnp.where(sub > js, change, 0.0)
+                    more = jnp.where(sub > js + 1, more, 0.0)
+                else:
+                    change = jnp.where(b < count - i, change + more, 0.0)
+                    more = 0.0
+                blocks[b] = blocks[b] - change - more
+        blocks = [pltpu.roll(block, LANES - SUB, 1) for block in blocks]
+        return blocks[1:] + blocks[:1]
+
+    blocks = lax.fori_loop(0, count, eight_rows, blocks)
+    blocks = [pltpu.roll(block, vectors, 1) for block in blocks]
     lefts, rights = [], []
     for b, block in enumerate(blocks):
         diagonal = jnp.sum(

time: 70 us -> 70.2 us (level)
  no operation moved by 1% of the time
where the time goes in v7:
time: 70.2 us; the launch traced here: 70.1 us
  Pallas kernels  69.4 us (99%)
    pallas_call x1, Pallas kernels, per_device(): pl.pallas_call(functools.partial(kernel, sizes), out_shape=(jax.ShapeDtyp...  63.1 us
    pallas_call x1, Pallas kernels, per_device(): pl.pallas_call(functools.partial(finish, sizes), out_shape=(jax.ShapeDtyp...  6.31 us

profile of v7, /device:TPU:0, one launch (start us, length us, event | category | flops | bytes accessed | tf_op | source)
XLA Modules:
  0.0 70.1 jit_solution(6409683096235193548)
XLA Ops:
  0.6 63.1 %shard_map.68 = (bf16[5,8,128,256]{3,2,1,0:T(8,128)(2,1)}, f32[8,128]{1,0:T(8,128)}) custom-call(f32[2560,128]{1,0:T(8,128)} %bitcast.1, f32[16,128]{1,0:T(8,128)} %va_ref.1, f32[16,128]{1,0:T(8,128)} %vr_ref.1, f32[5,5,16,128]{3,2,1,0:T(8,128)} %cp_ref.1, f32[5]{0:T(128)} %nu_ref.1), custom_call_target="tpu_custom_call" | custom-call | tf_op jit(solution)/shard_map/pallas_call | solution.py:425
  63.8 6.3 %shard_map.69 = (f32[32,5,16,128]{3,2,1,0:T(8,128)}, f32[32,32]{1,0:T(8,128)}) custom-call(f32[8,128]{1,0:T(8,128)} %get-tuple-element.4.folded_ref, bf16[5,8,128,256]{3,2,1,0:T(8,128)(2,1)} %get-tuple-element.5.split_in), custom_call_target="tpu_custom_call" | custom-call | tf_op jit(solution)/shard_map/pallas_call | solution.py:455
